TPU v7x, 32 devices: a whole 2x2x4 slice. The times are simulated.
32 devices in a mesh: pair: 8 (over y, x, core), virt: 4 (over z).
Axes of the slice: x: 2, y: 2, z: 4, core: 2. Of those that a mesh axis runs over, the one named last changes fastest.
Arguments:
- amps: bfloat16 [64, 1536, 1536], P('pair', 'virt'), may hold values from -6 to 6
- cycle_integrals: bfloat16 [1536, 1536], P('virt'), may hold values from -0.15625 to 0.15625
- mirror: int32 [64], replicated, may hold values from 0 to 63, as said below
- pair_list: int32 [64, 2], P('pair'), may hold values from 0 to 255, as said below
- tile_mask: int32 [64, 24], P('pair'), may hold values 0 or 1
- occ_energy: float32 [256], replicated, may hold values from -3 to -0.2
- virt_energy: float32 [1536], replicated, may hold values from 0.2 to 3
Outputs:
- update: bfloat16 [64, 1536, 1536], P('pair', 'virt')
Inputs may be any that keep to these rules, and one draw needn't show every extreme that they name: `mirror`: a permutation of the 64 pair slots; slot p lies on index p // 8 of pair; the partners of the 8 slots of index d lie one each on the indices (d + 1 + k * 1) mod 8 for k = 0 to 7; which slot of d goes to which of these indices, and the position inside that index, are drawn. `pair_list`: each row holds i and j with i not larger than j.
All inputs are finite; a program needn't handle non-finite values. No bound on the sum of `tile_mask` on one device may be relied on, other than what follows from the above.
Results may differ from a plain program's by a relative error of at most 0.0049.
Values may be sent and summed in bfloat16 or wider, within the bound.
No kernel may reach another device: no remote copies, remote signals or barrier semaphores. Data moves between devices by JAX's collectives and lax.ppermute only.
A program may use at most 128 MiB of HBM per device.

v0:
```python
import jax
import jax.numpy as jnp
from jax import lax
from jax.sharding import PartitionSpec as P

TILE = 64


def shifted(block, axis, distance):
    devices = range(lax.axis_size(axis))
    route = [((i - distance) % len(devices), i) for i in devices]
    return lax.ppermute(block, axis, route)


def send_partners(blocks, mirror, mover):
    devices = lax.axis_size("pair")
    here = lax.axis_index("pair")
    pair_dev = blocks.shape[0]
    stride = devices // pair_dev
    arrived = []
    for slot_k in range(pair_dev):
        offset = (1 + slot_k * stride) % devices
        receiver = (here - offset) % devices
        entries = lax.dynamic_slice_in_dim(mirror, receiver * pair_dev, pair_dev, 0)
        owned = entries // pair_dev == here
        wanted = jnp.sum(jnp.where(owned, entries - here * pair_dev, 0))
        chosen = lax.dynamic_index_in_dim(blocks, wanted, 0, keepdims=False)
        if offset == 0:
            arrived.append(chosen)
        else:
            arrived.append(mover(chosen, devices - offset))
    by_offset = jnp.stack(arrived, axis=0)
    own_entries = lax.dynamic_slice_in_dim(mirror, here * pair_dev, pair_dev, 0)
    order = (own_entries // pair_dev - here - 1) % devices // stride
    return jnp.take(by_offset, order, axis=0)


def fold_rows(stacked, piece):
    return jnp.einsum("prc,cb->prb", stacked, piece, preferred_element_type=jnp.float32)


def local(amps, cycle_integrals, mirror, pair_list, tile_mask, occ_energy, virt_energy):
    pair_dev, rows, width = amps.shape

    def move_amps(block, steps):
        return shifted(block, "pair", steps)

    partner_amps = send_partners(amps, mirror, move_amps)
    stacked = jnp.concatenate([amps, partner_amps], axis=0)
    summed = fold_rows(stacked, lax.all_gather(cycle_integrals, "virt", axis=0, tiled=True))
    contracted = summed.astype(jnp.bfloat16)
    own_part = contracted[:pair_dev]
    partner_part = contracted[pair_dev:]
    cycle = 2.0 * own_part.astype(jnp.float32) - partner_part.astype(jnp.float32)
    column = lax.axis_index("virt")
    lanes_all = jnp.repeat(tile_mask, TILE, axis=1).astype(jnp.float32)
    lanes_rows = lax.dynamic_slice_in_dim(lanes_all, column * rows, rows, 1)
    energy_rows = lax.dynamic_slice_in_dim(virt_energy, column * rows, rows, 0)
    orbitals = jnp.arange(occ_energy.shape[0], dtype=jnp.int32)
    first = jnp.sum(
        jnp.where(pair_list[:, 0:1] == orbitals[None, :], occ_energy[None, :], 0.0), axis=1
    )
    second = jnp.sum(
        jnp.where(pair_list[:, 1:2] == orbitals[None, :], occ_energy[None, :], 0.0), axis=1
    )
    occupied = first + second
    denom = (energy_rows[:, None] + virt_energy[None, :])[None, :, :] - occupied[:, None, None]
    result = cycle * lanes_rows[:, :, None] * lanes_all[:, None, :] / denom
    return result.astype(jnp.bfloat16)


def solution(mesh):
    return jax.shard_map(
        local,
        mesh=mesh,
        in_specs=(
            P("pair", "virt", None),
            P("virt", None),
            P(),
            P("pair", None),
            P("pair", None),
            P(),
            P(),
        ),
        out_specs=P("pair", "virt", None),
        check_vma=False,
    )
```

profile of v0, /device:TPU:0, one launch (start us, length us, event | category | flops | bytes accessed | tf_op | source)
XLA Modules:
  0.0 219.4 jit_solution(12580105732855294156)
XLA Ops:
  6.5 0.0 all-gather.2.cloned.1.call-start
  6.6 0.7 all-gather.2.cloned.1.call-update
  7.4 1.9 fusion.15
  22.2 6.7 %dynamic-slice_bitcast_fusion = (bf16[384,1536]{1,0:T(8,128)(2,1)}, bf16[384,1536]{1,0:T(8,128)(2,1)}, bf16[384,1536]{1,0:T(8,128)(2,1)}, bf16[384,1536]{1,0:T(8...) fusion(bf16[8,384,1536]{2,1,0:T(8,128)(2,1)} %param.7, ...), kind=kLoop, calls=%fused_computation.18 | loop fusion | bytes 16515100 | tf_op jit(solution)/shard_map/jit(dynamic_index_in_dim)/squeeze | solution.py:27
  29.0 3.3 %collective-permute-start = (bf16[384,1536]{1,0:T(8,128)(2,1)}, bf16[384,1536]{1,0:T(8,128)(2,1)}, u32[]{:S(2)}, u32[]{:S(2)}) collective-permute-start(bf16[384,1536]{1,0:T(8,128)(2,1)} %get-tuple-element.23), channel_id=1, source_target_pairs={{4,0},{8,4},{12,8},{16,12},{20,16},{24,20},{28,24},{0,28},{5,1},{9... | collective-permute-start | bytes 3538952 | tf_op jit(solution)/shard_map/ppermute | solution.py:12
  32.3 0.6 collective-permute-start.1
  32.9 0.3 collective-permute-start.2
  33.2 1.5 collective-permute-start.3
  34.7 0.1 collective-permute-start.4
  34.9 0.1 dynamic_slice.76
  34.9 0.6 compare_and_fusion
  35.5 0.8 select_reduce_fusion
  36.3 0.2 broadcast_add_fusion
  37.8 0.7 broadcast_in_dim.53
  38.5 1.6 convert_element_type.27
  40.8 1.2 add.164
  42.0 0.7 constant_dynamic-slice_fusion
  42.7 16.2 %collective-permute-done = bf16[384,1536]{1,0:T(8,128)(2,1)} collective-permute-done((bf16[384,1536]{1,0:T(8,128)(2,1)}, bf16[384,1536]{1,0:T(8,128)(2,1)}, u32[]{:S(2)}, u32[]{:S(2)}) %collective-permute-start) | collective-permute-done | bytes 1179680 | tf_op jit(solution)/shard_map/ppermute | solution.py:12
  58.9 2.4 %bitcast_dynamic-update-slice_fusion.6 = bf16[8,384,1536]{2,1,0:T(8,128)(2,1)} fusion(bf16[384,1536]{1,0:T(8,128)(2,1)} %collective-permute-done), kind=kLoop, calls=%fused_computation.15 | loop fusion | bytes 2359296
  61.3 23.0 %collective-permute-done.1 = bf16[384,1536]{1,0:T(8,128)(2,1)} collective-permute-done((bf16[384,1536]{1,0:T(8,128)(2,1)}, bf16[384,1536]{1,0:T(8,128)(2,1)}, u32[]{:S(2)}, u32[]{:S(2)}) %collective-permute-start.1) | collective-permute-done | bytes 1179680 | tf_op jit(solution)/shard_map/ppermute | solution.py:12
  84.3 2.4 %bitcast_dynamic-update-slice_fusion.5 = bf16[8,384,1536]{2,1,0:T(8,128)(2,1)} fusion(bf16[8,384,1536]{2,1,0:T(8,128)(2,1)} %bitcast_dynamic-update-slice_fusion.6, bf16[384,1536]{1,0:T(8,128)(2,1)} %collective-permute-done.1), kind=kLoop, calls=%fused_computation.14 | loop fusion | bytes 2359296
  86.7 2.4 %bitcast_dynamic-update-slice_fusion.4 = bf16[8,384,1536]{2,1,0:T(8,128)(2,1)} fusion(bf16[8,384,1536]{2,1,0:T(8,128)(2,1)} %bitcast_dynamic-update-slice_fusion.5, bf16[384,1536]{1,0:T(8,128)(2,1)} %collective-permute-done.2), kind=kLoop, calls=%fused_computation.13 | loop fusion | bytes 2359296
  89.1 48.0 %collective-permute-done.3 = bf16[384,1536]{1,0:T(8,128)(2,1)} collective-permute-done((bf16[384,1536]{1,0:T(8,128)(2,1)}, bf16[384,1536]{1,0:T(8,128)(2,1)}, u32[]{:S(2)}, u32[]{:S(2)}) %collective-permute-start.3) | collective-permute-done | bytes 1179680 | tf_op jit(solution)/shard_map/ppermute | solution.py:12
  137.0 2.4 %bitcast_dynamic-update-slice_fusion.3 = bf16[8,384,1536]{2,1,0:T(8,128)(2,1)} fusion(bf16[8,384,1536]{2,1,0:T(8,128)(2,1)} %bitcast_dynamic-update-slice_fusion.4, bf16[384,1536]{1,0:T(8,128)(2,1)} %collective-permute-done.3), kind=kLoop, calls=%fused_computation.12 | loop fusion | bytes 2359296
  139.4 1.1 bitcast_dynamic-update-slice_fusion.2
  140.5 1.1 bitcast_dynamic-update-slice_fusion.1
  141.6 1.1 bitcast_dynamic-update-slice_fusion
  142.7 2.4 %dynamic-slice_dynamic-update-slice_fusion = bf16[8,384,1536]{2,1,0:T(8,128)(2,1)} fusion(bf16[8,384,1536]{2,1,0:T(8,128)(2,1)} %bitcast_dynamic-update-slice_fusion, bf16[8,384,1536]{2,1,0:T(8,128)(2,1)} %param.7, s32[]{:T(128)S(6)} %select_n.210), kind=kLoop, calls=%fused_computation.17 | loop fusion | bytes 2359300 | tf_op jit(solution)/shard_map/stack | solution.py:32
  145.0 8.9 %gather_fusion = bf16[8,384,1536]{2,1,0:T(8,128)(2,1)} fusion(bf16[8,384,1536]{2,1,0:T(8,128)(2,1)} %dynamic-slice_dynamic-update-slice_fusion, s32[1024]{0:T(1024)S(1)} %pad_clamp_fusion), kind=kCustom, calls=%fused_computation | custom fusion | bytes 18874400 | tf_op jit(solution)/shard_map/jit(_take)/gather | solution.py:35
  153.9 8.4 %broadcast_select_fusion = bf16[8,384,1536]{2,1,0:T(8,128)(2,1)} fusion(bf16[8,384,1536]{2,1,0:T(8,128)(2,1)} %gather_fusion, pred[8]{0:T(512)(128)(4,1)S(1)} %copy-done.4), kind=kLoop, calls=%fused_computation.7 | loop fusion | flops 4718592 | bytes 18874376 | tf_op jit(solution)/shard_map/jit(_take)/select_n | solution.py:35
  162.3 36.1 %fusion.4 = bf16[16,384,1536]{2,1,0:T(8,128)(2,1)} fusion(bf16[8,384,1536]{2,1,0:T(8,128)(2,1)} %broadcast_select_fusion, bf16[8,384,1536]{2,1,0:T(8,128)(2,1)} %param.7, bf16[1536,1536]{1,0:T(8,128)(2,1)} %all-gather.2.cloned.1.call-done), kind=kOutput, calls=%fused_computation.6 | convolution fusion | flops 29009903616 | bytes 42467328 | tf_op jit(solution)/shard_map/prc,cb->prb/dot_general | solution.py:39
  198.4 14.1 %divide_convert_fusion = bf16[8,384,1536]{2,1,0:T(8,128)(2,1)} fusion(bf16[16,384,1536]{2,1,0:T(8,128)(2,1)} %fusion.4, f32[8]{0:T(128)S(1)} %copy-done.7, f32[384,1536]{1,0:T(8,128)S(1)} %broadcast_add_fusion, f32[8,1536]{1,0:T(8,128)S(1)} %copy-done, f32[8,384]{1,0:T(8,128)S(1)} %constant_dynamic-slice_fusion), kind=kLoop, calls=%fused_computation.5 | loop fusion | flops 42467328 | bytes 30732320 | tf_op jit(solution)/shard_map/convert_element_type | solution.py:69
  (26 shorter events, 0.1 us)
Async XLA Ops:
  6.5 28.4 %copy-start.1 = (s32[64]{0:T(128)S(1)}, s32[64]{0:T(128)}, u32[]{:S(2)}) copy-start(s32[64]{0:T(128)} %param.9) | copy-start | bytes 772
  6.5 28.3 %copy-start.2 = (f32[1536]{0:T(1024)S(1)}, f32[1536]{0:T(1024)}, u32[]{:S(2)}) copy-start(f32[1536]{0:T(1024)} %param.13) | copy-start | bytes 18436
  6.5 29.0 %copy-start.6 = (s32[8,2]{0,1:T(2,128)S(1)}, s32[8,2]{0,1:T(2,128)}, u32[]{:S(2)}) copy-start(s32[8,2]{0,1:T(2,128)} %param.10) | copy-start | bytes 196
  6.5 29.0 %copy-start.5 = (f32[256]{0:T(256)S(1)}, f32[256]{0:T(256)}, u32[]{:S(2)}) copy-start(f32[256]{0:T(256)} %param.12) | copy-start | bytes 3076
  6.5 155.8 %all-gather.2.cloned.1.call-start = ((), (), s32[]{:S(2)}) async-start(), calls=%async_computation | async-start | bytes 5898240 | tf_op jit(solution)/shard_map/all_gather | solution.py:50
  22.2 15.6 %copy-start.3 = (s32[8,24]{1,0:T(8,128)S(1)}, s32[8,24]{1,0:T(8,128)}, u32[]{:S(2)}) copy-start(s32[8,24]{1,0:T(8,128)} %param.11) | copy-start | bytes 2308
  29.0 29.9 %collective-permute-start = (bf16[384,1536]{1,0:T(8,128)(2,1)}, bf16[384,1536]{1,0:T(8,128)(2,1)}, u32[]{:S(2)}, u32[]{:S(2)}) collective-permute-start(bf16[384,1536]{1,0:T(8,128)(2,1)} %get-tuple-element.23), channel_id=1, source_target_pairs={{4,0},{8,4},{12,8},{16,12},{20,16},{24,20},{28,24},{0,28},{5,1},{9... | collective-permute-start | bytes 3538952 | tf_op jit(solution)/shard_map/ppermute | solution.py:12
  32.3 52.0 %collective-permute-start.1 = (bf16[384,1536]{1,0:T(8,128)(2,1)}, bf16[384,1536]{1,0:T(8,128)(2,1)}, u32[]{:S(2)}, u32[]{:S(2)}) collective-permute-start(bf16[384,1536]{1,0:T(8,128)(2,1)} %get-tuple-element.22), channel_id=1, source_target_pairs={{8,0},{12,4},{16,8},{20,12},{24,16},{28,20},{0,24},{4,28},{9,1},{1... | collective-permute-start | bytes 3538952 | tf_op jit(solution)/shard_map/ppermute | solution.py:12
  32.9 53.8 %collective-permute-start.2 = (bf16[384,1536]{1,0:T(8,128)(2,1)}, bf16[384,1536]{1,0:T(8,128)(2,1)}, u32[]{:S(2)}, u32[]{:S(2)}) collective-permute-start(bf16[384,1536]{1,0:T(8,128)(2,1)} %get-tuple-element.21), channel_id=1, source_target_pairs={{12,0},{16,4},{20,8},{24,12},{28,16},{0,20},{4,24},{8,28},{13,1},{... | collective-permute-start | bytes 3538952 | tf_op jit(solution)/shard_map/ppermute | solution.py:12
  33.2 103.8 %collective-permute-start.3 = (bf16[384,1536]{1,0:T(8,128)(2,1)}, bf16[384,1536]{1,0:T(8,128)(2,1)}, u32[]{:S(2)}, u32[]{:S(2)}) collective-permute-start(bf16[384,1536]{1,0:T(8,128)(2,1)} %get-tuple-element.20), channel_id=1, source_target_pairs={{16,0},{20,4},{24,8},{28,12},{0,16},{4,20},{8,24},{12,28},{17,1},{... | collective-permute-start | bytes 3538952 | tf_op jit(solution)/shard_map/ppermute | solution.py:12
  34.7 104.7 %collective-permute-start.4 = (bf16[384,1536]{1,0:T(8,128)(2,1)}, bf16[384,1536]{1,0:T(8,128)(2,1)S(1)}, u32[]{:S(2)}, u32[]{:S(2)}) collective-permute-start(bf16[384,1536]{1,0:T(8,128)(2,1)} %get-tuple-element.19), channel_id=1, source_target_pairs={{20,0},{24,4},{28,8},{0,12},{4,16},{8,20},{12,24},{16,28},{21,1},{... | collective-permute-start | bytes 3538952 | tf_op jit(solution)/shard_map/ppermute | solution.py:12
  58.9 81.6 %collective-permute-start.5 = (bf16[384,1536]{1,0:T(8,128)(2,1)}, bf16[384,1536]{1,0:T(8,128)(2,1)S(1)}, u32[]{:S(2)}, u32[]{:S(2)}) collective-permute-start(bf16[384,1536]{1,0:T(8,128)(2,1)} %get-tuple-element.18), channel_id=1, source_target_pairs={{24,0},{28,4},{0,8},{4,12},{8,16},{12,20},{16,24},{20,28},{25,1},{... | collective-permute-start | bytes 3538952 | tf_op jit(solution)/shard_map/ppermute | solution.py:12
  84.3 57.3 %collective-permute-start.6 = (bf16[384,1536]{1,0:T(8,128)(2,1)}, bf16[384,1536]{1,0:T(8,128)(2,1)S(1)}, u32[]{:S(2)}, u32[]{:S(2)}) collective-permute-start(bf16[384,1536]{1,0:T(8,128)(2,1)} %get-tuple-element.17), channel_id=1, source_target_pairs={{28,0},{0,4},{4,8},{8,12},{12,16},{16,20},{20,24},{24,28},{29,1},{... | collective-permute-start | bytes 3538952 | tf_op jit(solution)/shard_map/ppermute | solution.py:12
  145.0 8.9 %copy-start.4 = (pred[8]{0:T(512)(128)(4,1)S(1)}, pred[8]{0:T(512)(128)(4,1)}, u32[]{:S(2)}) copy-start(pred[8]{0:T(512)(128)(4,1)} %get-tuple-element.15) | copy-start | bytes 28
  162.3 36.1 %copy-start = (f32[8,1536]{1,0:T(8,128)S(1)}, f32[8,1536]{1,0:T(8,128)}, u32[]{:S(2)}) copy-start(f32[8,1536]{1,0:T(8,128)} %convert_element_type.27) | copy-start | bytes 147460
  162.3 36.1 %copy-start.7 = (f32[8]{0:T(128)S(1)}, f32[8]{0:T(128)}, u32[]{:S(2)}) copy-start(f32[8]{0:T(128)} %add.164) | copy-start | bytes 100
Sparse Core Ops, SparseCore 0:
  8.9 92.1 all-gather.1
where the time goes:
time: 220 us; the launch traced here: 219 us
  waiting for transfers between devices  87.9 us (40%)
  matrix products  36.1 us (16%)
  local copies, waits for them, and re-layouts  33.8 us (15%)
  between operations  28.5 us (13%)
  other arithmetic  27.2 us (12%)
  starting transfers between devices  5.91 us (3%)
    ppermute x7, waiting for transfers between devices, shifted(): return lax.ppermute(block, axis, route)  87.2 us
    dot_general x1, matrix products, fold_rows(): jnp.einsum('prc,cb->prb', stacked, piece, preferred_element_type=jnp.floa...  36.1 us
    convert_element_type x1, other arithmetic, local(): return result.astype(jnp.bfloat16)  14.1 us
    unnamed x23, local copies, waits for them, and re-layouts  12.7 us
    gather x1, local copies, waits for them, and re-layouts, send_partners(): return jnp.take(by_offset, order, axis=0)  8.86 us
    select_n x1, other arithmetic, send_partners(): return jnp.take(by_offset, order, axis=0)  8.39 us
    squeeze x1, local copies, waits for them, and re-layouts, send_partners(): chosen = lax.dynamic_index_in_dim(blocks, wanted, 0, keepdims=False)  6.75 us
    ppermute x7, starting transfers between devices, shifted(): return lax.ppermute(block, axis, route)  5.87 us
  transfers between devices with their start and end apart: 8, of which 3 were waited for; matrix products, arithmetic and copies ran while one was open for 21% of the time, Pallas kernels for 0%

commit v1 on v0

v1 whole, which is shorter than its diff:
```python
import functools

import jax
import jax.numpy as jnp
from jax import lax
from jax.experimental import pallas as pl
from jax.experimental.pallas import tpu as pltpu
from jax.sharding import PartitionSpec as P

TILE = 64
VMEM_BYTES = 24 * 1024 * 1024
FREE = pl.CostEstimate(flops=0, bytes_accessed=0, transcendentals=0)
ANY = pl.BlockSpec(memory_space=pl.ANY)
HBM = pl.BlockSpec(memory_space=pltpu.HBM)
WHOLE = pl.BlockSpec(memory_space=pltpu.VMEM)
SMEM = pl.BlockSpec(memory_space=pltpu.SMEM)


def in_hbm(array):
    return pltpu.with_memory_space_constraint(array, pltpu.HBM)


def in_vmem(array):
    return pltpu.with_memory_space_constraint(array, pltpu.VMEM)


def run_all(copies):
    for copy in copies:
        copy.start()
    for copy in copies:
        copy.wait()


def gate_kernel(*refs):
    del refs


def gate(values, earlier):
    count = len(values)
    return pl.pallas_call(
        gate_kernel,
        out_shape=[pltpu.HBM(value.shape, value.dtype) for value in values],
        in_specs=[ANY] * (count + len(earlier)),
        out_specs=[ANY] * count,
        input_output_aliases={n: n for n in range(count)},
        cost_estimate=FREE,
        name="gate",
    )(*[in_hbm(value) for value in values], *earlier)


def pick_kernel(parts, core_rows, *refs):
    slots_ref, amps_ref, shard_ref = refs[:3]
    outs, sems = refs[3:-1], refs[-1]
    copies = []
    for (steps, first, count), out in zip(parts, outs):
        for n, at in enumerate(steps):
            source = amps_ref.at[slots_ref[at], pl.ds(first, count)]
            copies.append(pltpu.make_async_copy(source, out.at[n], sems.at[len(copies)]))
    if core_rows:
        rows = pl.ds(slots_ref[slots_ref.shape[0] - 1] * core_rows, core_rows)
        copies.append(pltpu.make_async_copy(shard_ref.at[rows], outs[-1].at[0], sems.at[len(copies)]))
    run_all(copies)


def pick(parts, slots, amps, shard, core_rows=0, place=pltpu.VMEM):
    width = amps.shape[2]
    shapes = [place((len(steps), count, width), amps.dtype) for steps, _, count in parts]
    if core_rows:
        shapes.append(pltpu.HBM((1, core_rows, width), shard.dtype))
    return pl.pallas_call(
        functools.partial(pick_kernel, parts, core_rows),
        out_shape=shapes,
        in_specs=[SMEM, HBM, HBM],
        out_specs=[WHOLE] * len(shapes),
        scratch_shapes=[pltpu.SemaphoreType.DMA((sum(len(p[0]) for p in parts) + 1,))],
        compiler_params=pltpu.CompilerParams(vmem_limit_bytes=VMEM_BYTES),
        cost_estimate=FREE,
        name="pick",
    )(slots, in_hbm(amps), in_hbm(shard))


def assemble_kernel(crossing, count, place_ref, *refs):
    pieces, out_ref, sems = refs[:-2], refs[-2], refs[-1]
    z, core = place_ref[0], place_ref[1]
    copies = []
    for ref, first, mine in zip(pieces, *crossing):
        for n in range(ref.shape[0]):
            where = z ^ (first + n) if count == 4 else lax.rem(z + first + n, count)
            side = core if mine else 1 - core
            copies.append(pltpu.make_async_copy(ref.at[n], out_ref.at[where, side], sems.at[len(copies)]))
    run_all(copies)


def assemble(pieces, firsts, sides, place, count):
    _, half, width = pieces[0].shape
    full = pl.pallas_call(
        functools.partial(assemble_kernel, (firsts, sides), count),
        out_shape=pltpu.VMEM((count, 2, half, width), pieces[0].dtype),
        in_specs=[SMEM] + [ANY] * len(pieces),
        out_specs=WHOLE,
        scratch_shapes=[pltpu.SemaphoreType.DMA((2 * count,))],
        compiler_params=pltpu.CompilerParams(vmem_limit_bytes=VMEM_BYTES),
        cost_estimate=FREE,
        name="assemble",
    )(place, *map(in_hbm, pieces))
    return full.reshape(count * 2 * half, width)


def finish_kernel(whiches, owned, slots_ref, *refs):
    jobs = len(whiches)
    own_refs, refs = refs[:jobs if owned else 1], refs[jobs if owned else 1:]
    other_refs = refs[:jobs]
    k_ref, down_ref, across_ref = refs[jobs:jobs + 3]
    out_ref, mixed_ref = refs[-2:]
    step = pl.program_id(0)
    for job, (other_ref, which) in enumerate(zip(other_refs, whiches)):
        @pl.when(step == job)
        def _(job=job, other_ref=other_ref, which=which):
            own = own_refs[job if owned else 0][0]
            mixed_ref[...] = (own + own) - other_ref[which]

    cycle = jnp.dot(mixed_ref[...], k_ref[...], preferred_element_type=jnp.float32)
    denom = down_ref[0, :, 0:1] + across_ref[0, 0:1, :]
    kept = down_ref[0, :, 1:2] * across_ref[0, 1:2, :]
    out_ref[0] = (cycle * (kept / denom)).astype(out_ref.dtype)


def finish(first, jobs, slots, amps, integrals, down, across, so_far):
    pair_dev, _, width = amps.shape
    start, owns, others, whiches = zip(*jobs)
    owned = owns[0] is not None
    rows = others[0].shape[1]
    r = start[0] // rows
    own_specs = [WHOLE] * len(jobs) if owned else [pl.BlockSpec((1, rows, width), lambda n, s: (s[first + n], 0, 0))]
    in_specs = own_specs + [WHOLE] * (len(jobs) + 1) + [
        pl.BlockSpec((1, rows, 2), lambda n, s: (s[first + n], r, 0)),
        pl.BlockSpec((1, 2, width), lambda n, s: (s[first + n], 0, 0)),
    ]
    operands = [slots] + ([in_vmem(own) for own in owns] if owned else [in_hbm(amps)])
    operands += [in_vmem(other) if owned else other for other in others] + [in_vmem(integrals), down, across]
    aliases = {}
    if so_far is not None:
        aliases = {len(operands): 0}
        in_specs.append(ANY)
        operands.append(so_far)
    return pl.pallas_call(
        functools.partial(finish_kernel, whiches, owned),
        grid_spec=pltpu.PrefetchScalarGridSpec(
            num_scalar_prefetch=1,
            grid=(len(jobs),),
            in_specs=in_specs,
            out_specs=pl.BlockSpec((1, rows, width), lambda n, s: (s[first + n], r, 0)),
            scratch_shapes=[pltpu.VMEM((rows, width), jnp.bfloat16)],
        ),
        out_shape=jax.ShapeDtypeStruct(amps.shape, amps.dtype),
        input_output_aliases=aliases,
        compiler_params=pltpu.CompilerParams(vmem_limit_bytes=VMEM_BYTES),
        cost_estimate=FREE,
        name="finish",
    )(*operands)


def local(amps, cycle_integrals, mirror, pair_list, tile_mask, occ_energy, virt_energy):
    pair_dev, rows, width = amps.shape
    devices, planes = lax.axis_size("pair"), lax.axis_size("virt")
    here, column = lax.axis_index("pair"), lax.axis_index("virt")
    stride = devices // pair_dev
    crossing = stride == 1 and pair_dev == 8 and planes == 4
    order = [0, 1, 2, 4, 3, 5, 6, 7] if crossing else list(range(pair_dev))
    core = here % 2

    def move(block, axis, to):
        n = lax.axis_size(axis)
        return lax.ppermute(block, axis, [(i, to(i)) for i in range(n)])

    if crossing:
        target = source = here ^ jnp.array(order, dtype=jnp.int32)
    else:
        offsets = 1 + stride * jnp.arange(pair_dev, dtype=jnp.int32)
        target, source = (here - offsets) % devices, (here + offsets) % devices
    entries = mirror.reshape(devices, pair_dev)
    owner, inside = entries // pair_dev, entries % pair_dev
    place = jnp.arange(devices, dtype=jnp.int32)[None, :, None]
    slot = jnp.arange(pair_dev, dtype=jnp.int32)[None, None, :]
    target, source = target[:, None, None], source[:, None, None]
    outgoing = jnp.sum(jnp.where((place == target) & (owner[None] == here), inside[None], 0), axis=(1, 2))
    incoming = jnp.sum(jnp.where((place == here) & (owner[None] == source), slot, 0), axis=(1, 2))
    slots = jnp.concatenate([outgoing, incoming, core[None]]).astype(jnp.int32)

    def swap_cores(block):
        return move(block, "pair", lambda i: i ^ 1)

    core_rows = cycle_integrals.shape[0] // 2
    place = jnp.stack([column, core]).astype(jnp.int32)
    if crossing:
        cut = rows * 3 // 4
        out_at = {step: at for at, step in enumerate(order)}
        in_at = {step: pair_dev + at for at, step in enumerate(order)}
        to_x, to_y, to1, rows0 = pick(
            [((out_at[2], out_at[3]), 0, rows), ((out_at[4], out_at[5]), 0, rows), ((out_at[1],), 0, rows)],
            slots, amps, cycle_integrals, core_rows,
        )
        from_x = move(to_x, "pair", lambda i: i ^ 2)
        from_y = move(to_y, "pair", lambda i: i ^ 4)
        rows1, rows2 = move(rows0, "virt", lambda z: z ^ 1), move(rows0, "virt", lambda z: z ^ 2)
        rows3 = move(rows2, "virt", lambda z: z ^ 1)
        pieces = [rows0, rows1, rows2, rows3]
        pieces += [swap_cores(piece) for piece in pieces]
        integrals = assemble(pieces, [0, 1, 2, 3] * 2, [1] * 4 + [0] * 4, place, planes)
        from1 = swap_cores(to1)
        at6, at7 = (out_at[6],), (out_at[7],)
        in6, in7 = (in_at[6],), (in_at[7],)
        to0, to6, to7a, to7b = pick(
            [((out_at[0],), 0, rows), (at6, 0, rows), (at7, 0, cut), (at7, cut, rows - cut)],
            slots, amps, cycle_integrals, place=pltpu.HBM,
        )
        to6, to7a, to7b, from_x, from_y = gate([to6, to7a, to7b, from_x, from_y], [*pieces, from1])
        own6, own7a, own7b = pick(
            [(in6, 0, rows), (in7, 0, cut), (in7, cut, rows - cut)], slots, amps, cycle_integrals
        )
        from6, from7a, from7b = [move(block, "pair", lambda i, j=j: i ^ j) for j, block in ((6, to6), (7, to7a), (7, to7b))]
        swap_x, swap_y = swap_cores(from_x), swap_cores(from_y)
        calls = [
            [(0, None, to0, 0), (0, None, from1, 0), (0, None, from_x, 0), (0, None, from_y, 0)],
            [(0, None, swap_x, 1), (0, None, swap_y, 1)],
            [(0, own6, from6, 0)],
            [(0, own7a, from7a, 0)],
            [(cut, own7b, from7b, 0)],
        ]
        firsts = [in_at[0], in_at[3], in_at[6], in_at[7], in_at[7]]
    else:
        *to_all, rows0 = pick([((k,), 0, rows) for k in range(pair_dev)], slots, amps, cycle_integrals, core_rows)
        mine = [rows0] + [move(rows0, "virt", lambda z, s=s: (z - s) % planes) for s in range(1, planes)]
        other = [swap_cores(piece) for piece in mine]
        integrals = assemble(
            mine + other, 2 * list(range(planes)), [1] * planes + [0] * planes, place, planes
        )
        calls, firsts = [], []
        for k in range(pair_dev):
            arrived = move(to_all[k], "pair", lambda i, k=k: (i - 1 - k * stride) % devices)
            calls.append([(0, None, arrived, 0)])
            firsts.append(pair_dev + k)

    lanes = jnp.repeat(tile_mask, TILE, axis=1).astype(jnp.float32)
    lanes_rows = lax.dynamic_slice_in_dim(lanes, column * rows, rows, 1)
    energy_rows = lax.dynamic_slice_in_dim(virt_energy, column * rows, rows, 0)
    orbitals = jnp.arange(occ_energy.shape[0], dtype=jnp.int32)
    first = jnp.sum(jnp.where(pair_list[:, 0:1] == orbitals[None, :], occ_energy[None, :], 0.0), axis=1)
    second = jnp.sum(jnp.where(pair_list[:, 1:2] == orbitals[None, :], occ_energy[None, :], 0.0), axis=1)
    occupied = first + second
    down = jnp.stack([energy_rows[None, :] - occupied[:, None], lanes_rows], axis=-1)
    across = jnp.stack([jnp.broadcast_to(virt_energy[None, :], lanes.shape), lanes], axis=1)

    result = None
    for first_slot, jobs in zip(firsts, calls):
        result = finish(first_slot, jobs, slots, amps, integrals, down, across, result)
    return result


def solution(mesh):
    return jax.shard_map(
        local,
        mesh=mesh,
        in_specs=(
            P("pair", "virt", None),
            P("virt", None),
            P(),
            P("pair", None),
            P("pair", None),
            P(),
            P(),
        ),
        out_specs=P("pair", "virt", None),
        check_vma=False,
    )
```

time: 220 us -> 120 us (0.55)
  Pallas kernels: 0 us -> 45.4 us
  waiting for transfers between devices: 87.9 us -> 50.2 us
  matrix products: 36.1 us -> 0 us
  between operations: 28.5 us -> 0.33 us
  local copies, waits for them, and re-layouts: 33.8 us -> 5.84 us
  other arithmetic: 27.2 us -> 1.76 us
  starting transfers between devices: 5.91 us -> 15.6 us
    pallas_call x0 -> x10, Pallas kernels: none -> 45.4 us  [the longest x5 31.5 us: finish(): pl.pallas_call(functools.partial(finish_kernel, whiches, owned), grid_spe...]
    ppermute x7 -> x15, waiting for transfers between devices: 87.2 us -> 50.2 us  [move(): return lax.ppermute(block, axis, [(i, to(i)) for i in range(n)])]
    dot_general x1 -> x0, matrix products: 36.1 us -> none  [fold_rows(): jnp.einsum('prc,cb->prb', stacked, piece, preferred_element_type=jnp.floa...]
    convert_element_type x2 -> x1, other arithmetic: 14.1 us -> 0.01 us  [local(): lanes = jnp.repeat(tile_mask, TILE, axis=1).astype(jnp.float32)]
    ppermute x7 -> x15, starting transfers between devices: 5.87 us -> 15.6 us  [move(): return lax.ppermute(block, axis, [(i, to(i)) for i in range(n)])]
    gather x1 -> x0, local copies, waits for them, and re-layouts: 8.86 us -> none  [send_partners(): return jnp.take(by_offset, order, axis=0)]
    unnamed x23 -> x42, local copies, waits for them, and re-layouts: 12.7 us -> 4.2 us
    select_n x1, other arithmetic: 8.39 us -> 0.01 us  [local(): owner, inside = (entries // pair_dev, entries % pair_dev)]
  transfers between devices with their start and end apart: 8 -> 15, of which waited for: 3 -> 6; matrix products, arithmetic and copies ran while one was open for 21% -> 1% of each run, Pallas kernels for 0% -> 33%
where the time goes in v1:
time: 120 us; the launch traced here: 119 us
  waiting for transfers between devices  50.2 us (42%)
  Pallas kernels  45.4 us (38%)
  starting transfers between devices  15.6 us (13%)
  local copies, waits for them, and re-layouts  5.84 us (5%)
  other arithmetic  1.76 us (1%)
    ppermute x15, waiting for transfers between devices, move(): return lax.ppermute(block, axis, [(i, to(i)) for i in range(n)])  50.2 us
    pallas_call x5, Pallas kernels, finish(): pl.pallas_call(functools.partial(finish_kernel, whiches, owned), grid_spe...  31.5 us
    ppermute x15, starting transfers between devices, move(): return lax.ppermute(block, axis, [(i, to(i)) for i in range(n)])  15.6 us
    pallas_call x3, Pallas kernels, pick(): pl.pallas_call(functools.partial(pick_kernel, parts, core_rows), out_shap...  10.7 us
    unnamed x42, local copies, waits for them, and re-layouts  4.2 us
    pallas_call x1, Pallas kernels, assemble(): pl.pallas_call(functools.partial(assemble_kernel, (firsts, sides), count)...  3.21 us
  transfers between devices with their start and end apart: 15, of which 6 were waited for; matrix products, arithmetic and copies ran while one was open for 1% of the time, Pallas kernels for 33%

profile of v1, /device:TPU:0, one launch (start us, length us, event | category | flops | bytes accessed | tf_op | source)
XLA Modules:
  0.0 119.1 jit_solution(1928383653770387099)
XLA Ops:
  0.0 0.7 reshape.158
  0.8 0.7 broadcast_xor_fusion
  1.5 0.4 select_reduce_fusion
  2.0 4.3 %pick.5 = (bf16[2,384,1536]{2,1,0:T(8,128)(2,1)S(1)}, bf16[2,384,1536]{2,1,0:T(8,128)(2,1)S(1)}, bf16[1,384,1536]{2,1,0:T(8,128)(2,1)S(1)}, bf16[1,192,1536]{2,1,0:T(8,128)(2,1)}) custom-call(s32[17]{0:T(128)S(1)} %pad_add_fusion.refs_0_.slots_ref, bf16[8,384,1536]{2,1,0:T(8,128)(2,1)} %refs_0_.3, bf16[384,1536]{1,0:T(8,128)(2,1)} %refs_2_.5), custom_call_target="tpu_custom_call" | custom-call | tf_op jit(solution)/shard_map/pick/pallas_call | solution.py:70
  6.3 3.0 %collective-permute-start = (bf16[2,384,1536]{2,1,0:T(8,128)(2,1)S(1)}, bf16[2,384,1536]{2,1,0:T(8,128)(2,1)S(1)}, u32[]{:S(2)}, u32[]{:S(2)}) collective-permute-start(bf16[2,384,1536]{2,1,0:T(8,128)(2,1)S(1)} %get-tuple-element.25), channel_id=1, source_target_pairs={{0,8},{4,12},{8,0},{12,4},{16,24},{20,28},{24,16},{28,20},{1,9},{5... | collective-permute-start | bytes 7077896 | tf_op jit(solution)/shard_map/ppermute | solution.py:174
  9.3 1.5 %collective-permute-start.1 = (bf16[2,384,1536]{2,1,0:T(8,128)(2,1)S(1)}, bf16[2,384,1536]{2,1,0:T(8,128)(2,1)}, u32[]{:S(2)}, u32[]{:S(2)}) collective-permute-start(bf16[2,384,1536]{2,1,0:T(8,128)(2,1)S(1)} %get-tuple-element.26), channel_id=1, source_target_pairs={{0,16},{4,20},{8,24},{12,28},{16,0},{20,4},{24,8},{28,12},{1,17},{... | collective-permute-start | bytes 7077896 | tf_op jit(solution)/shard_map/ppermute | solution.py:174
  10.9 2.6 %collective-permute-start.3 = (bf16[1,192,1536]{2,1,0:T(8,128)(2,1)}, bf16[1,192,1536]{2,1,0:T(8,128)(2,1)S(1)}, u32[]{:S(2)}, u32[]{:S(2)}) collective-permute-start(bf16[1,192,1536]{2,1,0:T(8,128)(2,1)} %get-tuple-element.27.refs_5_.refs_0_), channel_id=1, source_target_pairs={{0,2},{1,3},{2,0},{3,1},{4,6},{5,7},{6,4},{7,5},{8,10},{9,11},{10,... | collective-permute-start | bytes 1769480 | tf_op jit(solution)/shard_map/ppermute | solution.py:174
  13.4 1.6 %collective-permute-start.2 = (bf16[1,192,1536]{2,1,0:T(8,128)(2,1)}, bf16[1,192,1536]{2,1,0:T(8,128)(2,1)S(1)}, u32[]{:S(2)}, u32[]{:S(2)}) collective-permute-start(bf16[1,192,1536]{2,1,0:T(8,128)(2,1)} %get-tuple-element.27.refs_5_.refs_0_), channel_id=1, source_target_pairs={{0,1},{1,0},{2,3},{3,2},{4,5},{5,4},{6,7},{7,6},{8,9},{9,8},{10,11... | collective-permute-start | bytes 1769480 | tf_op jit(solution)/shard_map/ppermute | solution.py:174
  15.0 24.2 %collective-permute-done.3.refs_7_.refs_2_ = bf16[1,192,1536]{2,1,0:T(8,128)(2,1)S(1)} collective-permute-done((bf16[1,192,1536]{2,1,0:T(8,128)(2,1)}, bf16[1,192,1536]{2,1,0:T(8,128)(2,1)S(1)}, u32[]{:S(2)}, u32[]{:S(2)}) %collective-permute-start.3) | collective-permute-done | bytes 589856 | tf_op jit(solution)/shard_map/ppermute | solution.py:174
  39.4 1.4 %collective-permute-start.4 = (bf16[1,192,1536]{2,1,0:T(8,128)(2,1)S(1)}, bf16[1,192,1536]{2,1,0:T(8,128)(2,1)S(1)}, u32[]{:S(2)}, u32[]{:S(2)}) collective-permute-start(bf16[1,192,1536]{2,1,0:T(8,128)(2,1)S(1)} %collective-permute-done.3.refs_7_.refs_2_), channel_id=1, source_target_pairs={{0,1},{1,0},{2,3},{3,2},{4,5},{5,4},{6,7},{7,6},{8,9},{9,8},{10,11... | collective-permute-start | bytes 1769480 | tf_op jit(solution)/shard_map/ppermute | solution.py:174
  40.8 14.1 %collective-permute-done.4.refs_8_.refs_3_ = bf16[1,192,1536]{2,1,0:T(8,128)(2,1)S(1)} collective-permute-done((bf16[1,192,1536]{2,1,0:T(8,128)(2,1)S(1)}, bf16[1,192,1536]{2,1,0:T(8,128)(2,1)S(1)}, u32[]{:S(2)}, u32[]{:S(2)}) %collective-permute-start.4) | collective-permute-done | bytes 589856 | tf_op jit(solution)/shard_map/ppermute | solution.py:174
  55.0 0.9 copy-done.13
  55.9 0.4 collective-permute-start.8
  56.3 4.3 %pick.4 = (bf16[1,384,1536]{2,1,0:T(8,128)(2,1)}, bf16[1,384,1536]{2,1,0:T(8,128)(2,1)}, bf16[1,288,1536]{2,1,0:T(8,128)(2,1)}, bf16[1,96,1536]{2,1,0:T(8,128)(2,1)}) custom-call(s32[17]{0:T(128)S(1)} %pad_add_fusion.refs_0_.slots_ref, bf16[8,384,1536]{2,1,0:T(8,128)(2,1)} %refs_0_.3, bf16[384,1536]{1,0:T(8,128)(2,1)} %refs_2_.5), custom_call_target="tpu_custom_call" | custom-call | tf_op jit(solution)/shard_map/pick/pallas_call | solution.py:70
  60.7 1.4 %collective-permute-done.1.refs_4_ = bf16[2,384,1536]{2,1,0:T(8,128)(2,1)} collective-permute-done((bf16[2,384,1536]{2,1,0:T(8,128)(2,1)S(1)}, bf16[2,384,1536]{2,1,0:T(8,128)(2,1)}, u32[]{:S(2)}, u32[]{:S(2)}) %collective-permute-start.1) | collective-permute-done | bytes 2359328 | tf_op jit(solution)/shard_map/ppermute | solution.py:174
  62.1 0.8 copy-done
  63.0 0.4 collective-permute-start.14
  63.4 1.8 %collective-permute-start.12 = (bf16[1,384,1536]{2,1,0:T(8,128)(2,1)}, bf16[1,384,1536]{2,1,0:T(8,128)(2,1)S(1)}, u32[]{:S(2)}, u32[]{:S(2)}) collective-permute-start(bf16[1,384,1536]{2,1,0:T(8,128)(2,1)} %get-tuple-element.33), channel_id=1, source_target_pairs={{0,24},{4,28},{8,16},{12,20},{16,8},{20,12},{24,0},{28,4},{1,25},{... | collective-permute-start | bytes 3538952 | tf_op jit(solution)/shard_map/ppermute | solution.py:174
  65.6 2.2 %pick.3 = (bf16[1,384,1536]{2,1,0:T(8,128)(2,1)S(1)}, bf16[1,288,1536]{2,1,0:T(8,128)(2,1)S(1)}, bf16[1,96,1536]{2,1,0:T(8,128)(2,1)S(1)}) custom-call(s32[17]{0:T(128)S(1)} %pad_add_fusion.refs_0_.slots_ref, bf16[8,384,1536]{2,1,0:T(8,128)(2,1)} %refs_0_.3, bf16[384,1536]{1,0:T(8,128)(2,1)} %refs_2_.5), custom_call_target="tpu_custom_call" | custom-call | tf_op jit(solution)/shard_map/pick/pallas_call | solution.py:70
  67.8 1.0 copy-done.5
  68.8 0.9 copy-done.7
  69.8 0.6 collective-permute-start.11
  70.7 0.5 copy.28.refs_6_.refs_4_.refs_3_
  71.2 2.2 %collective-permute-start.10 = (bf16[1,96,1536]{2,1,0:T(8,128)(2,1)S(1)}, bf16[1,96,1536]{2,1,0:T(8,128)(2,1)S(1)}, u32[]{:S(2)}, u32[]{:S(2)}) collective-permute-start(bf16[1,96,1536]{2,1,0:T(8,128)(2,1)S(1)} %copy-done.16), channel_id=1, source_target_pairs={{0,28},{4,24},{8,20},{12,16},{16,12},{20,8},{24,4},{28,0},{1,29},{... | collective-permute-start | bytes 884744 | tf_op jit(solution)/shard_map/ppermute | solution.py:174
  73.6 3.2 %assemble.1 = bf16[4,2,192,1536]{3,2,1,0:T(8,128)(2,1)S(1)} custom-call(s32[2]{0:T(128)S(1)} %pad_add_fusion.1.place_ref, bf16[1,192,1536]{2,1,0:T(8,128)(2,1)} %get-tuple-element.27.refs_5_.refs_0_, bf16[1,192,1536]{2,1,0:T(8,128)(2,1)} %copy-done.10, bf16[1,192,1536]{2,1,0:T(8,128)(2,1)} %copy-done.9, bf16[1,192,1536]{2,1,0:T(8,128)(2,1)} %copy-done.12, ...), custom_call_target="tpu_custom_call" | custom-call | tf_op jit(solution)/shard_map/assemble/pallas_call | solution.py:96
  77.3 12.7 %finish.5.refs_6_ = bf16[8,384,1536]{2,1,0:T(8,128)(2,1)} custom-call(s32[17]{0:T(128)S(1)} %pad_add_fusion.refs_0_.slots_ref, bf16[8,384,1536]{2,1,0:T(8,128)(2,1)} %refs_0_.3, bf16[1,384,1536]{2,1,0:T(8,128)(2,1)S(1)} %copy-done.4, bf16[1,384,1536]{2,1,0:T(8,128)(2,1)S(1)} %copy-done.3, bf16[2,384,1536]{2,1,0:T(8,128)(2,1)S(1)} %copy-done.1, ...), custom_call_target="tpu_custom_call" | custom-call | tf_op jit(solution)/shard_map/finish/pallas_call | solution.py:146
  90.1 8.7 %finish.6.refs_5_ = bf16[8,384,1536]{2,1,0:T(8,128)(2,1)} custom-call(s32[17]{0:T(128)S(1)} %pad_add_fusion.refs_0_.slots_ref, bf16[8,384,1536]{2,1,0:T(8,128)(2,1)} %refs_0_.3, bf16[2,384,1536]{2,1,0:T(8,128)(2,1)} %collective-permute-done.13.refs_1_, bf16[2,384,1536]{2,1,0:T(8,128)(2,1)} %collective-permute-done.14.refs_2_, ...), custom_call_target="tpu_custom_call", output_to_operand_aliasing={{}: (7, {})} | custom-call | tf_op jit(solution)/shard_map/finish/pallas_call | solution.py:146
  98.8 3.6 %finish.7.refs_5_ = bf16[8,384,1536]{2,1,0:T(8,128)(2,1)} custom-call(s32[17]{0:T(128)S(1)} %pad_add_fusion.refs_0_.slots_ref, bf16[1,384,1536]{2,1,0:T(8,128)(2,1)S(1)} %copy-done.6, bf16[1,384,1536]{2,1,0:T(8,128)(2,1)S(1)} %collective-permute-done.12.refs_1_, bf16[1536,1536]{1,0:T(8,128)(2,1)S(1)} %bitcast.11, ...), custom_call_target="tpu_custom_call", output_to_operand_aliasing={{}: (6, {})} | custom-call | tf_op jit(solution)/shard_map/finish/pallas_call | solution.py:146
  102.4 8.4 %collective-permute-done.11.refs_1_ = bf16[1,288,1536]{2,1,0:T(8,128)(2,1)} collective-permute-done((bf16[1,288,1536]{2,1,0:T(8,128)(2,1)}, bf16[1,288,1536]{2,1,0:T(8,128)(2,1)}, u32[]{:S(2)}, u32[]{:S(2)}) %collective-permute-start.11) | collective-permute-done | bytes 884768 | tf_op jit(solution)/shard_map/ppermute | solution.py:174
  110.9 4.2 %finish.8.refs_5_ = bf16[8,384,1536]{2,1,0:T(8,128)(2,1)} custom-call(s32[17]{0:T(128)S(1)} %pad_add_fusion.refs_0_.slots_ref, bf16[1,288,1536]{2,1,0:T(8,128)(2,1)S(1)} %copy-done.8, bf16[1,288,1536]{2,1,0:T(8,128)(2,1)} %collective-permute-done.11.refs_1_, bf16[1536,1536]{1,0:T(8,128)(2,1)S(1)} %bitcast.12, ...), custom_call_target="tpu_custom_call", output_to_operand_aliasing={{}: (6, {})} | custom-call | tf_op jit(solution)/shard_map/finish/pallas_call | solution.py:146
  115.1 1.9 %collective-permute-done.10.refs_1_ = bf16[1,96,1536]{2,1,0:T(8,128)(2,1)S(1)} collective-permute-done((bf16[1,96,1536]{2,1,0:T(8,128)(2,1)S(1)}, bf16[1,96,1536]{2,1,0:T(8,128)(2,1)S(1)}, u32[]{:S(2)}, u32[]{:S(2)}) %collective-permute-start.10) | collective-permute-done | bytes 294944 | tf_op jit(solution)/shard_map/ppermute | solution.py:174
  117.0 2.2 %finish.9 = bf16[8,384,1536]{2,1,0:T(8,128)(2,1)} custom-call(s32[17]{0:T(128)S(1)} %pad_add_fusion.refs_0_.slots_ref, bf16[1,96,1536]{2,1,0:T(8,128)(2,1)S(1)} %get-tuple-element.21.refs_0_, bf16[1,96,1536]{2,1,0:T(8,128)(2,1)S(1)} %collective-permute-done.10.refs_1_, bf16[1536,1536]{1,0:T(8,128)(2,1)S(1)} %bitcast.13, ...), custom_call_target="tpu_custom_call", output_to_operand_aliasing={{}: (6, {})} | custom-call | tf_op jit(solution)/shard_map/finish/pallas_call | solution.py:146
  (73 shorter events, 1.9 us)
Async XLA Ops:
  6.3 54.4 %collective-permute-start = (bf16[2,384,1536]{2,1,0:T(8,128)(2,1)S(1)}, bf16[2,384,1536]{2,1,0:T(8,128)(2,1)S(1)}, u32[]{:S(2)}, u32[]{:S(2)}) collective-permute-start(bf16[2,384,1536]{2,1,0:T(8,128)(2,1)S(1)} %get-tuple-element.25), channel_id=1, source_target_pairs={{0,8},{4,12},{8,0},{12,4},{16,24},{20,28},{24,16},{28,20},{1,9},{5... | collective-permute-start | bytes 7077896 | tf_op jit(solution)/shard_map/ppermute | solution.py:174
  9.3 52.8 %collective-permute-start.1 = (bf16[2,384,1536]{2,1,0:T(8,128)(2,1)S(1)}, bf16[2,384,1536]{2,1,0:T(8,128)(2,1)}, u32[]{:S(2)}, u32[]{:S(2)}) collective-permute-start(bf16[2,384,1536]{2,1,0:T(8,128)(2,1)S(1)} %get-tuple-element.26), channel_id=1, source_target_pairs={{0,16},{4,20},{8,24},{12,28},{16,0},{20,4},{24,8},{28,12},{1,17},{... | collective-permute-start | bytes 7077896 | tf_op jit(solution)/shard_map/ppermute | solution.py:174
  10.9 28.3 %collective-permute-start.3 = (bf16[1,192,1536]{2,1,0:T(8,128)(2,1)}, bf16[1,192,1536]{2,1,0:T(8,128)(2,1)S(1)}, u32[]{:S(2)}, u32[]{:S(2)}) collective-permute-start(bf16[1,192,1536]{2,1,0:T(8,128)(2,1)} %get-tuple-element.27.refs_5_.refs_0_), channel_id=1, source_target_pairs={{0,2},{1,3},{2,0},{3,1},{4,6},{5,7},{6,4},{7,5},{8,10},{9,11},{10,... | collective-permute-start | bytes 1769480 | tf_op jit(solution)/shard_map/ppermute | solution.py:174
  13.4 25.9 %collective-permute-start.2 = (bf16[1,192,1536]{2,1,0:T(8,128)(2,1)}, bf16[1,192,1536]{2,1,0:T(8,128)(2,1)S(1)}, u32[]{:S(2)}, u32[]{:S(2)}) collective-permute-start(bf16[1,192,1536]{2,1,0:T(8,128)(2,1)} %get-tuple-element.27.refs_5_.refs_0_), channel_id=1, source_target_pairs={{0,1},{1,0},{2,3},{3,2},{4,5},{5,4},{6,7},{7,6},{8,9},{9,8},{10,11... | collective-permute-start | bytes 1769480 | tf_op jit(solution)/shard_map/ppermute | solution.py:174
  15.0 25.8 %collective-permute-start.5 = (bf16[1,192,1536]{2,1,0:T(8,128)(2,1)}, bf16[1,192,1536]{2,1,0:T(8,128)(2,1)S(1)}, u32[]{:S(2)}, u32[]{:S(2)}) collective-permute-start(bf16[1,192,1536]{2,1,0:T(8,128)(2,1)} %get-tuple-element.27.refs_5_.refs_0_), channel_id=1, source_target_pairs={{0,4},{4,0},{8,12},{12,8},{16,20},{20,16},{24,28},{28,24},{1,5},{5... | collective-permute-start | bytes 1769480 | tf_op jit(solution)/shard_map/ppermute | solution.py:174
  39.2 21.4 %copy-start.9 = (bf16[1,192,1536]{2,1,0:T(8,128)(2,1)}, bf16[1,192,1536]{2,1,0:T(8,128)(2,1)S(1)}, u32[]{:S(2)}) copy-start(bf16[1,192,1536]{2,1,0:T(8,128)(2,1)S(1)} %collective-permute-done.3.refs_7_.refs_2_) | copy-start | bytes 1769476
  39.2 21.5 %collective-permute-start.9 = (bf16[1,384,1536]{2,1,0:T(8,128)(2,1)S(1)}, bf16[1,384,1536]{2,1,0:T(8,128)(2,1)S(1)}, u32[]{:S(2)}, u32[]{:S(2)}) collective-permute-start(bf16[1,384,1536]{2,1,0:T(8,128)(2,1)S(1)} %get-tuple-element.28), channel_id=1, source_target_pairs={{0,4},{4,0},{8,12},{12,8},{16,20},{20,16},{24,28},{28,24},{1,5},{5... | collective-permute-start | bytes 3538952 | tf_op jit(solution)/shard_map/ppermute | solution.py:174
  39.4 15.6 %copy-start.10 = (bf16[1,192,1536]{2,1,0:T(8,128)(2,1)}, bf16[1,192,1536]{2,1,0:T(8,128)(2,1)S(1)}, u32[]{:S(2)}) copy-start(bf16[1,192,1536]{2,1,0:T(8,128)(2,1)S(1)} %collective-permute-done.2.refs_6_.refs_1_) | copy-start | bytes 1769476
  39.4 15.6 %collective-permute-start.4 = (bf16[1,192,1536]{2,1,0:T(8,128)(2,1)S(1)}, bf16[1,192,1536]{2,1,0:T(8,128)(2,1)S(1)}, u32[]{:S(2)}, u32[]{:S(2)}) collective-permute-start(bf16[1,192,1536]{2,1,0:T(8,128)(2,1)S(1)} %collective-permute-done.3.refs_7_.refs_2_), channel_id=1, source_target_pairs={{0,1},{1,0},{2,3},{3,2},{4,5},{5,4},{6,7},{7,6},{8,9},{9,8},{10,11... | collective-permute-start | bytes 1769480 | tf_op jit(solution)/shard_map/ppermute | solution.py:174
  40.8 14.1 %copy-start.11 = (bf16[1,192,1536]{2,1,0:T(8,128)(2,1)}, bf16[1,192,1536]{2,1,0:T(8,128)(2,1)S(1)}, u32[]{:S(2)}) copy-start(bf16[1,192,1536]{2,1,0:T(8,128)(2,1)S(1)} %collective-permute-done.5.refs_9_.refs_4_) | copy-start | bytes 1769476
  40.8 14.1 %collective-permute-start.6 = (bf16[1,192,1536]{2,1,0:T(8,128)(2,1)S(1)}, bf16[1,192,1536]{2,1,0:T(8,128)(2,1)S(1)}, u32[]{:S(2)}, u32[]{:S(2)}) collective-permute-start(bf16[1,192,1536]{2,1,0:T(8,128)(2,1)S(1)} %collective-permute-done.2.refs_6_.refs_1_), channel_id=1, source_target_pairs={{0,4},{4,0},{8,12},{12,8},{16,20},{20,16},{24,28},{28,24},{1,5},{5... | collective-permute-start | bytes 1769480 | tf_op jit(solution)/shard_map/ppermute | solution.py:174
  55.0 5.7 %copy-start.12 = (bf16[1,192,1536]{2,1,0:T(8,128)(2,1)}, bf16[1,192,1536]{2,1,0:T(8,128)(2,1)S(1)}, u32[]{:S(2)}) copy-start(bf16[1,192,1536]{2,1,0:T(8,128)(2,1)S(1)} %collective-permute-done.4.refs_8_.refs_3_) | copy-start | bytes 1769476
  55.0 5.7 %collective-permute-start.7 = (bf16[1,192,1536]{2,1,0:T(8,128)(2,1)S(1)}, bf16[1,192,1536]{2,1,0:T(8,128)(2,1)S(1)}, u32[]{:S(2)}, u32[]{:S(2)}) collective-permute-start(bf16[1,192,1536]{2,1,0:T(8,128)(2,1)S(1)} %collective-permute-done.3.refs_7_.refs_2_), channel_id=1, source_target_pairs={{0,4},{4,0},{8,12},{12,8},{16,20},{20,16},{24,28},{28,24},{1,5},{5... | collective-permute-start | bytes 1769480 | tf_op jit(solution)/shard_map/ppermute | solution.py:174
  55.9 4.8 %collective-permute-start.8 = (bf16[1,192,1536]{2,1,0:T(8,128)(2,1)S(1)}, bf16[1,192,1536]{2,1,0:T(8,128)(2,1)S(1)}, u32[]{:S(2)}, u32[]{:S(2)}) collective-permute-start(bf16[1,192,1536]{2,1,0:T(8,128)(2,1)S(1)} %collective-permute-done.4.refs_8_.refs_3_), channel_id=1, source_target_pairs={{0,4},{4,0},{8,12},{12,8},{16,20},{20,16},{24,28},{28,24},{1,5},{5... | collective-permute-start | bytes 1769480 | tf_op jit(solution)/shard_map/ppermute | solution.py:174
  60.7 1.5 %copy-start.14 = (bf16[1,192,1536]{2,1,0:T(8,128)(2,1)}, bf16[1,192,1536]{2,1,0:T(8,128)(2,1)S(1)}, u32[]{:S(2)}) copy-start(bf16[1,192,1536]{2,1,0:T(8,128)(2,1)S(1)} %collective-permute-done.7.refs_11_.refs_6_) | copy-start | bytes 1769476
  60.7 1.5 %copy-start.2 = (bf16[1,384,1536]{2,1,0:T(8,128)(2,1)}, bf16[1,384,1536]{2,1,0:T(8,128)(2,1)S(1)}, u32[]{:S(2)}) copy-start(bf16[1,384,1536]{2,1,0:T(8,128)(2,1)S(1)} %collective-permute-done.9.refs_13_.refs_2_) | copy-start | bytes 3538948
  60.7 2.2 %copy-start = (bf16[2,384,1536]{2,1,0:T(8,128)(2,1)}, bf16[2,384,1536]{2,1,0:T(8,128)(2,1)S(1)}, u32[]{:S(2)}) copy-start(bf16[2,384,1536]{2,1,0:T(8,128)(2,1)S(1)} %collective-permute-done.refs_3_) | copy-start | bytes 7077892
  62.9 2.3 %copy-start.18 = (s32[8,24]{1,0:T(8,128)S(1)}, s32[8,24]{1,0:T(8,128)}, u32[]{:S(2)}) copy-start(s32[8,24]{1,0:T(8,128)} %param.12) | copy-start | bytes 2308
  62.9 27.1 %collective-permute-start.13 = (bf16[2,384,1536]{2,1,0:T(8,128)(2,1)}, bf16[2,384,1536]{2,1,0:T(8,128)(2,1)}, u32[]{:S(2)}, u32[]{:S(2)}) collective-permute-start(bf16[2,384,1536]{2,1,0:T(8,128)(2,1)} %get-tuple-element.34.refs_3_), channel_id=1, source_target_pairs={{0,4},{4,0},{8,12},{12,8},{16,20},{20,16},{24,28},{28,24},{1,5},{5... | collective-permute-start | bytes 7077896 | tf_op jit(solution)/shard_map/ppermute | solution.py:174
  63.0 27.0 %collective-permute-start.14 = (bf16[2,384,1536]{2,1,0:T(8,128)(2,1)}, bf16[2,384,1536]{2,1,0:T(8,128)(2,1)}, u32[]{:S(2)}, u32[]{:S(2)}) collective-permute-start(bf16[2,384,1536]{2,1,0:T(8,128)(2,1)} %get-tuple-element.35.refs_4_), channel_id=1, source_target_pairs={{0,4},{4,0},{8,12},{12,8},{16,20},{20,16},{24,28},{28,24},{1,5},{5... | collective-permute-start | bytes 7077896 | tf_op jit(solution)/shard_map/ppermute | solution.py:174
  63.4 35.3 %collective-permute-start.12 = (bf16[1,384,1536]{2,1,0:T(8,128)(2,1)}, bf16[1,384,1536]{2,1,0:T(8,128)(2,1)S(1)}, u32[]{:S(2)}, u32[]{:S(2)}) collective-permute-start(bf16[1,384,1536]{2,1,0:T(8,128)(2,1)} %get-tuple-element.33), channel_id=1, source_target_pairs={{0,24},{4,28},{8,16},{12,20},{16,8},{20,12},{24,0},{28,4},{1,25},{... | collective-permute-start | bytes 3538952 | tf_op jit(solution)/shard_map/ppermute | solution.py:174
  65.6 4.2 %copy-start.17 = (f32[1536]{0:T(1024)S(1)}, f32[1536]{0:T(1024)}, u32[]{:S(2)}) copy-start(f32[1536]{0:T(1024)} %param.14) | copy-start | bytes 18436
  65.6 4.2 %copy-start.20 = (s32[8,2]{0,1:T(2,128)S(1)}, s32[8,2]{0,1:T(2,128)}, u32[]{:S(2)}) copy-start(s32[8,2]{0,1:T(2,128)} %param.11) | copy-start | bytes 196
  65.6 4.8 %copy-start.19 = (f32[256]{0:T(256)S(1)}, f32[256]{0:T(256)}, u32[]{:S(2)}) copy-start(f32[256]{0:T(256)} %param.13) | copy-start | bytes 3076
  65.6 5.6 %copy-start.16 = (bf16[1,96,1536]{2,1,0:T(8,128)(2,1)S(1)}, bf16[1,96,1536]{2,1,0:T(8,128)(2,1)}, u32[]{:S(2)}) copy-start(bf16[1,96,1536]{2,1,0:T(8,128)(2,1)} %get-tuple-element.29) | copy-start | bytes 884740
  69.8 41.1 %collective-permute-start.11 = (bf16[1,288,1536]{2,1,0:T(8,128)(2,1)}, bf16[1,288,1536]{2,1,0:T(8,128)(2,1)}, u32[]{:S(2)}, u32[]{:S(2)}) collective-permute-start(bf16[1,288,1536]{2,1,0:T(8,128)(2,1)} %get-tuple-element.31), channel_id=1, source_target_pairs={{0,28},{4,24},{8,20},{12,16},{16,12},{20,8},{24,4},{28,0},{1,29},{... | collective-permute-start | bytes 2654216 | tf_op jit(solution)/shard_map/ppermute | solution.py:174
  71.2 45.7 %collective-permute-start.10 = (bf16[1,96,1536]{2,1,0:T(8,128)(2,1)S(1)}, bf16[1,96,1536]{2,1,0:T(8,128)(2,1)S(1)}, u32[]{:S(2)}, u32[]{:S(2)}) collective-permute-start(bf16[1,96,1536]{2,1,0:T(8,128)(2,1)S(1)} %copy-done.16), channel_id=1, source_target_pairs={{0,28},{4,24},{8,20},{12,16},{16,12},{20,8},{24,4},{28,0},{1,29},{... | collective-permute-start | bytes 884744 | tf_op jit(solution)/shard_map/ppermute | solution.py:174
  73.6 3.3 %copy-start.1 = (bf16[2,384,1536]{2,1,0:T(8,128)(2,1)S(1)}, bf16[2,384,1536]{2,1,0:T(8,128)(2,1)}, u32[]{:S(2)}) copy-start(bf16[2,384,1536]{2,1,0:T(8,128)(2,1)} %get-tuple-element.34.refs_3_) | copy-start | bytes 7077892
  73.6 3.4 %copy-start.3 = (bf16[1,384,1536]{2,1,0:T(8,128)(2,1)S(1)}, bf16[1,384,1536]{2,1,0:T(8,128)(2,1)}, u32[]{:S(2)}) copy-start(bf16[1,384,1536]{2,1,0:T(8,128)(2,1)} %copy-done.2) | copy-start | bytes 3538948
  73.6 3.7 %copy-start.4 = (bf16[1,384,1536]{2,1,0:T(8,128)(2,1)S(1)}, bf16[1,384,1536]{2,1,0:T(8,128)(2,1)}, u32[]{:S(2)}) copy-start(bf16[1,384,1536]{2,1,0:T(8,128)(2,1)} %get-tuple-element.36.refs_1_) | copy-start | bytes 3538948
  90.1 8.7 %copy-start.6 = (bf16[1,384,1536]{2,1,0:T(8,128)(2,1)S(1)}, bf16[1,384,1536]{2,1,0:T(8,128)(2,1)}, u32[]{:S(2)}) copy-start(bf16[1,384,1536]{2,1,0:T(8,128)(2,1)} %copy-done.5) | copy-start | bytes 3538948
  98.8 12.1 %copy-start.8 = (bf16[1,288,1536]{2,1,0:T(8,128)(2,1)S(1)}, bf16[1,288,1536]{2,1,0:T(8,128)(2,1)}, u32[]{:S(2)}) copy-start(bf16[1,288,1536]{2,1,0:T(8,128)(2,1)} %copy-done.7) | copy-start | bytes 2654212
  (4 other events, 4.3 us)

commit v2 on v1

v2 whole, which is shorter than its diff:
```python
import functools

import jax
import jax.numpy as jnp
from jax import lax
from jax.experimental import pallas as pl
from jax.experimental.pallas import tpu as pltpu
from jax.sharding import PartitionSpec as P

TILE = 64
VMEM_BYTES = 16 * 1024 * 1024
PIECES = 3
FREE = pl.CostEstimate(flops=0, bytes_accessed=0, transcendentals=0)
ANY = pl.BlockSpec(memory_space=pl.ANY)
HBM = pl.BlockSpec(memory_space=pltpu.HBM)
WHOLE = pl.BlockSpec(memory_space=pltpu.VMEM)
SMEM = pl.BlockSpec(memory_space=pltpu.SMEM)


def in_hbm(array):
    return pltpu.with_memory_space_constraint(array, pltpu.HBM)


def in_vmem(array):
    return pltpu.with_memory_space_constraint(array, pltpu.VMEM)


def run_all(copies):
    for copy in copies:
        copy.start()
    for copy in copies:
        copy.wait()


def pick_kernel(picks, core_rows, pair_dev, waits, *refs):
    mirror_ref, amps_ref, shard_ref = refs[:3]
    outs, sems = refs[3 + waits:-1], refs[-1]
    here = lax.axis_index("pair")
    copies = []

    def slot_of(peer, outgoing):
        found = jnp.int32(0)
        for e in range(pair_dev):
            entry = mirror_ref[(peer if outgoing else here) * pair_dev + e]
            if pair_dev & (pair_dev - 1) == 0:
                owner = lax.shift_right_logical(entry, jnp.int32(pair_dev.bit_length() - 1))
                inside = entry & (pair_dev - 1)
            else:
                owner = lax.div(entry, jnp.int32(pair_dev))
                inside = lax.rem(entry, jnp.int32(pair_dev))
            value = inside if outgoing else jnp.int32(e)
            found = found + jnp.where(owner == (here if outgoing else peer), value, 0)
        return found

    for (parts, outgoing), out in zip(picks, outs):
        done = 0
        for peer, first, count in parts:
            slot = slot_of(peer(here), outgoing)
            for at in range(0, count, count // PIECES):
                size = count // PIECES
                source = amps_ref.at[slot, pl.ds(first + at, size)]
                copies.append(pltpu.make_async_copy(source, out.at[0, pl.ds(done + at, size)], sems.at[len(copies)]))
                copies[-1].start()
            done += count
    if core_rows:
        rows = pl.ds((here & 1) * core_rows, core_rows)
        copies.append(pltpu.make_async_copy(shard_ref.at[rows], outs[-1].at[0], sems.at[len(copies)]))
        copies[-1].start()
    for copy in copies:
        copy.wait()


def pick(picks, mirror, amps, shard, core_rows=0, place=pltpu.VMEM, earlier=()):
    pair_dev, _, width = amps.shape
    shapes = [place((1, sum(p[2] for p in parts), width), amps.dtype) for parts, _ in picks]
    if core_rows:
        shapes.append(place((1, core_rows, width), shard.dtype))
    return pl.pallas_call(
        functools.partial(pick_kernel, picks, core_rows, pair_dev, len(earlier)),
        out_shape=shapes,
        in_specs=[SMEM, HBM, HBM] + [ANY] * len(earlier),
        out_specs=[WHOLE] * len(shapes),
        scratch_shapes=[pltpu.SemaphoreType.DMA((PIECES * sum(len(parts) for parts, _ in picks) + 1,))],
        compiler_params=pltpu.CompilerParams(vmem_limit_bytes=VMEM_BYTES),
        cost_estimate=FREE,
        name="pick",
    )(mirror, in_hbm(amps), in_hbm(shard), *earlier)


def extract_kernel(parts, *refs):
    out_ref, sems = refs[-2:]
    copies, done = [], 0
    for n, (start, count) in enumerate(parts):
        source, target = refs[n].at[0, pl.ds(start, count)], out_ref.at[0, pl.ds(done, count)]
        copies.append(pltpu.make_async_copy(source, target, sems.at[n]))
        done += count
    run_all(copies)


def extract(parts, earlier=()):
    arrays = [array for array, _, _ in parts]
    rows, width = sum(count for _, _, count in parts), arrays[0].shape[2]
    return pl.pallas_call(
        functools.partial(extract_kernel, [part[1:] for part in parts]),
        out_shape=pltpu.VMEM((1, rows, width), arrays[0].dtype),
        in_specs=[ANY] * (len(arrays) + len(earlier)),
        out_specs=WHOLE,
        scratch_shapes=[pltpu.SemaphoreType.DMA((len(parts),))],
        compiler_params=pltpu.CompilerParams(vmem_limit_bytes=VMEM_BYTES),
        cost_estimate=FREE,
        name="extract",
    )(*arrays, *earlier)


def assemble_kernel(crossing, count, place_ref, *refs):
    pieces, out_ref, sems = refs[:-2], refs[-2], refs[-1]
    z, core = place_ref[0], place_ref[1]
    copies = []
    for ref, first, mine in zip(pieces, *crossing):
        for n in range(ref.shape[0]):
            where = z ^ (first + n) if count == 4 else lax.rem(z + first + n, count)
            side = core if mine else 1 - core
            copies.append(pltpu.make_async_copy(ref.at[n], out_ref.at[where, side], sems.at[len(copies)]))
    run_all(copies)


def assemble(pieces, firsts, sides, place, count):
    _, half, width = pieces[0].shape
    full = pl.pallas_call(
        functools.partial(assemble_kernel, (firsts, sides), count),
        out_shape=pltpu.VMEM((count, 2, half, width), pieces[0].dtype),
        in_specs=[SMEM] + [ANY] * len(pieces),
        out_specs=WHOLE,
        scratch_shapes=[pltpu.SemaphoreType.DMA((2 * count,))],
        compiler_params=pltpu.CompilerParams(vmem_limit_bytes=VMEM_BYTES),
        cost_estimate=FREE,
        name="assemble",
    )(place, *map(in_hbm, pieces))
    return full.reshape(count * 2 * half, width)


def finish_kernel(jobs, owned, slots_ref, *refs):
    own_ref, refs = refs[0], refs[1:]
    count = sum(map(len, jobs))
    other_refs, (k_ref, down_ref, across_ref) = list(refs[:count]), refs[count:count + 3]
    out_ref, token_ref, mixed_ref = refs[-3:]
    step = pl.program_id(0)
    token_ref[...] = jnp.zeros_like(token_ref)
    for job, lengths in enumerate(jobs):
        parts = [(other_refs.pop(0), length) for length in lengths]

        @pl.when(step == job)
        def _(parts=parts):
            first = 0
            for other_ref, length in parts:
                rows = pl.ds(first, length)
                own = own_ref[0, rows]
                mixed_ref[rows] = (own + own) - other_ref[0]
                first += length

    cycle = jnp.dot(mixed_ref[...], k_ref[...], preferred_element_type=jnp.float32)
    denom = down_ref[0, :, 0:1] + across_ref[0, 0:1, :]
    kept = down_ref[0, :, 1:2] * across_ref[0, 1:2, :]
    out_ref[0] = (cycle * (kept / denom)).astype(out_ref.dtype)


def finish(first, first_row, jobs, slots, amps, integrals, down, across, so_far, own=None):
    _, _, width = amps.shape
    rows = sum(length for _, _, length in jobs[0])
    r = first_row // rows
    others = [other for job in jobs for other, _, _ in job]
    in_specs = [pl.BlockSpec((1, rows, width), lambda n, s: (s[first + n], r, 0)) if own is None else WHOLE]
    for job in jobs:
        for _, start, length in job:
            in_specs.append(pl.BlockSpec((1, length, width), lambda n, s, at=start // length: (0, at, 0)))
    in_specs += [
        WHOLE,
        pl.BlockSpec((1, rows, 2), lambda n, s: (s[first + n], r, 0)),
        pl.BlockSpec((1, 2, width), lambda n, s: (s[first + n], 0, 0)),
    ]
    operands = [slots, in_hbm(amps) if own is None else in_vmem(own)]
    operands += others + [in_vmem(integrals), down, across]
    aliases = {}
    if so_far is not None:
        aliases = {len(operands): 0}
        in_specs.append(ANY)
        operands.append(so_far)
    return pl.pallas_call(
        functools.partial(finish_kernel, [[length for _, _, length in job] for job in jobs], own is not None),
        grid_spec=pltpu.PrefetchScalarGridSpec(
            num_scalar_prefetch=1,
            grid=(len(jobs),),
            in_specs=in_specs,
            out_specs=[
                pl.BlockSpec((1, rows, width), lambda n, s: (s[first + n], r, 0)),
                pl.BlockSpec((8, 128), lambda n, s: (0, 0)),
            ],
            scratch_shapes=[pltpu.VMEM((rows, width), jnp.bfloat16)],
        ),
        out_shape=[jax.ShapeDtypeStruct(amps.shape, amps.dtype), jax.ShapeDtypeStruct((8, 128), jnp.float32)],
        input_output_aliases=aliases,
        compiler_params=pltpu.CompilerParams(vmem_limit_bytes=VMEM_BYTES),
        cost_estimate=FREE,
        name="finish",
    )(*operands)


def finish_together_kernel(first, first_row, jobs, columns, slots_ref, *refs):
    count = len(jobs)
    rows = sum(length for _, length in jobs[0])
    own_refs, refs = refs[:count], refs[count:]
    parts = sum(map(len, jobs))
    other_refs, (k_ref, down_ref, across_ref) = list(refs[:parts]), refs[parts:parts + 3]
    out_ref, mixed_ref, done_ref, sems = refs[-4:]
    for job, lengths in enumerate(jobs):
        at = 0
        for start, length in lengths:
            other_ref = other_refs.pop(0)
            own = own_refs[job][0, pl.ds(at, length)]
            mixed_ref[pl.ds(job * rows + at, length)] = (own + own) - other_ref[0, pl.ds(start, length)]
            at += length
    copies = []
    for n in range(out_ref.shape[2] // columns):
        part = pl.ds(n * columns, columns)
        cycle = jnp.dot(mixed_ref[...], k_ref[:, part], preferred_element_type=jnp.float32)
        for job in range(count):
            slot = slots_ref[first + job]
            mine, here = pl.ds(job * rows, rows), pl.ds(first_row, rows)
            denom = down_ref[slot, here, 0:1] + across_ref[slot, 0:1, part]
            kept = down_ref[slot, here, 1:2] * across_ref[slot, 1:2, part]
            done_ref[mine, part] = (cycle[job * rows:(job + 1) * rows] * (kept / denom)).astype(done_ref.dtype)
            target = out_ref.at[slot, here, part]
            copies.append(pltpu.make_async_copy(done_ref.at[mine, part], target, sems.at[len(copies)]))
            copies[-1].start()
    for copy in copies:
        copy.wait()


def finish_together(first, first_row, jobs, slots, owns, integrals, down, across, so_far, columns=512):
    width = integrals.shape[1]
    rows = sum(length for _, _, length in jobs[0])
    others = [other for job in jobs for other, _, _ in job]
    steps = width // columns
    operands = [slots, *map(in_vmem, owns), *others, in_vmem(integrals), down, across, so_far]
    return pl.pallas_call(
        functools.partial(
            finish_together_kernel, first, first_row, [[part[1:] for part in job] for job in jobs], columns
        ),
        in_specs=[SMEM] + [WHOLE] * (len(operands) - 2) + [ANY],
        out_specs=ANY,
        out_shape=jax.ShapeDtypeStruct(so_far.shape, so_far.dtype),
        scratch_shapes=[
            pltpu.VMEM((len(jobs) * rows, width), jnp.bfloat16),
            pltpu.VMEM((len(jobs) * rows, width), jnp.bfloat16),
            pltpu.SemaphoreType.DMA((steps * len(jobs),)),
        ],
        input_output_aliases={len(operands) - 1: 0},
        compiler_params=pltpu.CompilerParams(vmem_limit_bytes=VMEM_BYTES),
        cost_estimate=FREE,
        name="finish_together",
    )(*operands)


def local(amps, cycle_integrals, mirror, pair_list, tile_mask, occ_energy, virt_energy):
    pair_dev, rows, width = amps.shape
    devices, planes = lax.axis_size("pair"), lax.axis_size("virt")
    here, column = lax.axis_index("pair"), lax.axis_index("virt")
    stride = devices // pair_dev
    crossing = stride == 1 and pair_dev == 8 and planes == 4
    order = [0, 1, 6, 7, 2, 4, 3, 5] if crossing else list(range(pair_dev))
    core = here % 2

    def move(block, axis, to):
        n = lax.axis_size(axis)
        return lax.ppermute(block, axis, [(i, to(i)) for i in range(n)])

    if crossing:
        source = here ^ jnp.array(order, dtype=jnp.int32)
    else:
        source = (here + 1 + stride * jnp.arange(pair_dev, dtype=jnp.int32)) % devices
    entries = lax.dynamic_slice_in_dim(mirror, here * pair_dev, pair_dev, 0)
    slot = jnp.arange(pair_dev, dtype=jnp.int32)
    slots = jnp.sum(jnp.where(entries[None, :] // pair_dev == source[:, None], slot[None, :], 0), axis=1)

    def swap_cores(block):
        return move(block, "pair", lambda i: i ^ 1)

    lanes = jnp.repeat(tile_mask, TILE, axis=1).astype(jnp.float32)
    lanes_rows = lax.dynamic_slice_in_dim(lanes, column * rows, rows, 1)
    energy_rows = lax.dynamic_slice_in_dim(virt_energy, column * rows, rows, 0)
    orbitals = jnp.arange(occ_energy.shape[0], dtype=jnp.int32)
    first = jnp.sum(jnp.where(pair_list[:, 0:1] == orbitals[None, :], occ_energy[None, :], 0.0), axis=1)
    second = jnp.sum(jnp.where(pair_list[:, 1:2] == orbitals[None, :], occ_energy[None, :], 0.0), axis=1)
    occupied = first + second
    down = jnp.stack([energy_rows[None, :] - occupied[:, None], lanes_rows], axis=-1)
    across = jnp.stack([jnp.broadcast_to(virt_energy[None, :], lanes.shape), lanes], axis=1)

    def run(first, first_row, jobs, integrals, so_far):
        return finish(first, first_row, jobs, slots, amps, integrals, down, across, so_far)

    core_rows = cycle_integrals.shape[0] // 2
    place = jnp.stack([column, core]).astype(jnp.int32)
    if crossing:
        in_at = {step: at for at, step in enumerate(order)}
        quarter = rows // 4

        def peer(step):
            return lambda i: i ^ step

        def take(parts, earlier=(), outgoing=True, core_rows=0, place=pltpu.VMEM):
            picks = [([(peer(step), first, count) for step, first, count in part], outgoing) for part in parts]
            return pick(picks, mirror, amps, cycle_integrals, core_rows, place, earlier)

        def shift(value, step):
            return move(value, "pair", peer(step))

        def whole(step):
            return (step, 0, rows)

        def quarters(step, first, count):
            return (step, first * quarter, count * quarter)

        to_d, to1, rows0 = take([[whole(6), whole(7)], [whole(1)]], core_rows=core_rows)
        from_d, from1 = shift(to_d, 6), swap_cores(to1)
        rows1, rows2 = move(rows0, "virt", lambda z: z ^ 1), move(rows0, "virt", lambda z: z ^ 2)
        rows3 = move(rows2, "virt", lambda z: z ^ 1)
        pieces = [rows0, rows1, rows2, rows3]
        pieces += [swap_cores(piece) for piece in pieces]
        integrals = assemble(pieces, [0, 1, 2, 3] * 2, [1] * 4 + [0] * 4, place, planes)
        to_x, to_y = take(
            [[whole(2), quarters(3, 0, 1)], [whole(4), quarters(5, 0, 1)]], [rows1, rows2, slots, down, across]
        )
        from_x, from_y = shift(to_x, 2), shift(to_y, 4)
        to0, = take([[whole(0)]], [rows1])
        tails = take([[quarters(3, 1, 2)], [quarters(5, 1, 2)]], [from_d])
        from3, from5 = shift(tails[0], 3), shift(tails[1], 5)
        swap_d = swap_cores(extract([(from_d, rows, rows)]))
        parts = [[(part, 0, rows)] for part in (to0, from1, from_d, swap_d)]
        result, done = run(0, 0, parts, integrals, None)
        last = take([[quarters(3, 3, 1)], [quarters(5, 3, 1)]], [from_d])
        owns = take([[whole(2)], [whole(4)]], [from_d], False)
        owns += take([[quarters(s, *q)] for q in ((0, 3), (3, 1)) for s in (3, 5)], [from_d], False)
        swapped = swap_cores(extract([(from_x, rows, quarter), (from_y, rows, quarter)], [done, *last, *owns]))
        last3, last5 = shift(last[0], 3), shift(last[1], 5)

        def together(first, first_row, parts, owns, so_far):
            return finish_together(first, first_row, parts, slots, owns, integrals, down, across, so_far)

        parts = [[(from_x, 0, rows)], [(from_y, 0, rows)]]
        result = together(in_at[2], 0, parts, owns[:2], result)
        parts = [[(swapped, n * quarter, quarter), (direct, 0, 2 * quarter)] for n, direct in enumerate((from3, from5))]
        result = together(in_at[3], 0, parts, owns[2:4], result)
        parts = [[(last3, 0, quarter)], [(last5, 0, quarter)]]
        result = together(in_at[3], 3 * quarter, parts, owns[4:], result)
    else:
        picks = []
        for k in range(pair_dev):
            offset = (1 + k * stride) % devices
            picks.append(([(lambda i, o=offset: lax.rem(i + devices - o, jnp.int32(devices)), 0, rows)], True))
        *to_all, rows0 = pick(picks, mirror, amps, cycle_integrals, core_rows, pltpu.HBM)
        mine = [rows0] + [move(rows0, "virt", lambda z, s=s: (z - s) % planes) for s in range(1, planes)]
        other = [swap_cores(piece) for piece in mine]
        integrals = assemble(
            mine + other, 2 * list(range(planes)), [1] * planes + [0] * planes, place, planes
        )
        result = None
        for k in range(pair_dev):
            arrived = move(to_all[k], "pair", lambda i, k=k: (i - 1 - k * stride) % devices)
            result, _ = run(k, 0, [[(arrived, 0, rows)]], integrals, result)
    return result


def solution(mesh):
    return jax.shard_map(
        local,
        mesh=mesh,
        in_specs=(
            P("pair", "virt", None),
            P("virt", None),
            P(),
            P("pair", None),
            P("pair", None),
            P(),
            P(),
        ),
        out_specs=P("pair", "virt", None),
        check_vma=False,
    )
```

time: 120 us -> 114 us (0.950)
  waiting for transfers between devices: 50.2 us -> 43.5 us
  Pallas kernels: 45.4 us -> 49.6 us
    ppermute x15 -> x17, waiting for transfers between devices: 50.2 us -> 43.5 us  [move(): return lax.ppermute(block, axis, [(i, to(i)) for i in range(n)])]
    pallas_call x9 -> x13, Pallas kernels: 42.2 us -> 46.7 us  [the longest x7 18.9 us: pick(): pl.pallas_call(functools.partial(pick_kernel, picks, core_rows, pair_dev,...]
    unnamed x42 -> x22, local copies, waits for them, and re-layouts: 4.2 us -> 2.89 us
    ppermute x15 -> x17, starting transfers between devices: 15.6 us -> 14.7 us  [move(): return lax.ppermute(block, axis, [(i, to(i)) for i in range(n)])]
  transfers between devices with their start and end apart: 15 -> 17, of which waited for: 6 -> 7; matrix products, arithmetic and copies ran while one was open for 1% -> 2% of each run, Pallas kernels for 33% -> 37%
where the time goes in v2:
time: 114 us
  Pallas kernels  49.6 us (44%)
  waiting for transfers between devices  43.5 us (38%)
  starting transfers between devices  14.7 us (13%)
  local copies, waits for them, and re-layouts  5 us (4%)
    ppermute x17, waiting for transfers between devices, move(): return lax.ppermute(block, axis, [(i, to(i)) for i in range(n)])  43.5 us
    pallas_call x7, Pallas kernels, pick(): pl.pallas_call(functools.partial(pick_kernel, picks, core_rows, pair_dev,...  18.9 us
    ppermute x17, starting transfers between devices, move(): return lax.ppermute(block, axis, [(i, to(i)) for i in range(n)])  14.7 us
    pallas_call x3, Pallas kernels, finish_together(): pl.pallas_call(functools.partial(finish_together_kernel, first, first_row...  13.2 us
    pallas_call x1, Pallas kernels, finish(): pl.pallas_call(functools.partial(finish_kernel, [[length for _, _, length...  12.3 us
    pallas_call x1, Pallas kernels, assemble(): pl.pallas_call(functools.partial(assemble_kernel, (firsts, sides), count)...  2.93 us
    unnamed x22, local copies, waits for them, and re-layouts  2.89 us
    pallas_call x2, Pallas kernels, extract(): pl.pallas_call(functools.partial(extract_kernel, [part[1:] for part in pa...  2.33 us
  transfers between devices with their start and end apart: 17, of which 7 were waited for; matrix products, arithmetic and copies ran while one was open for 2% of the time, Pallas kernels for 37%

profile of v2, /device:TPU:0, one launch (start us, length us, event | category | flops | bytes accessed | tf_op | source)
XLA Modules:
  0.0 113.7 jit_solution(6641748780536838650)
XLA Ops:
  0.0 0.7 copy-done.3
  0.7 4.8 %pick.7 = (bf16[1,768,1536]{2,1,0:T(8,128)(2,1)}, bf16[1,384,1536]{2,1,0:T(8,128)(2,1)}, bf16[1,192,1536]{2,1,0:T(8,128)(2,1)}) custom-call(s32[64]{0:T(128)S(1)} %copy-done.3, bf16[8,384,1536]{2,1,0:T(8,128)(2,1)} %refs_1_.13, bf16[384,1536]{1,0:T(8,128)(2,1)} %refs_2_.13), custom_call_target="tpu_custom_call" | custom-call | tf_op jit(solution)/shard_map/pick/pallas_call | solution.py:78
  5.5 4.0 %collective-permute-start = (bf16[1,768,1536]{2,1,0:T(8,128)(2,1)}, bf16[1,768,1536]{2,1,0:T(8,128)(2,1)S(1)}, u32[]{:S(2)}, u32[]{:S(2)}) collective-permute-start(bf16[1,768,1536]{2,1,0:T(8,128)(2,1)} %get-tuple-element.22), channel_id=1, source_target_pairs={{0,24},{4,28},{8,16},{12,20},{16,8},{20,12},{24,0},{28,4},{1,25},{... | collective-permute-start | bytes 7077896 | tf_op jit(solution)/shard_map/ppermute | solution.py:275
  9.4 2.6 %collective-permute-start.4 = (bf16[1,192,1536]{2,1,0:T(8,128)(2,1)}, bf16[1,192,1536]{2,1,0:T(8,128)(2,1)}, u32[]{:S(2)}, u32[]{:S(2)}) collective-permute-start(bf16[1,192,1536]{2,1,0:T(8,128)(2,1)} %get-tuple-element.27.refs_0_), channel_id=1, source_target_pairs={{0,2},{1,3},{2,0},{3,1},{4,6},{5,7},{6,4},{7,5},{8,10},{9,11},{10,... | collective-permute-start | bytes 1769480 | tf_op jit(solution)/shard_map/ppermute | solution.py:275
  12.0 1.6 %collective-permute-start.3 = (bf16[1,192,1536]{2,1,0:T(8,128)(2,1)}, bf16[1,192,1536]{2,1,0:T(8,128)(2,1)S(1)}, u32[]{:S(2)}, u32[]{:S(2)}) collective-permute-start(bf16[1,192,1536]{2,1,0:T(8,128)(2,1)} %get-tuple-element.27.refs_0_), channel_id=1, source_target_pairs={{0,1},{1,0},{2,3},{3,2},{4,5},{5,4},{6,7},{7,6},{8,9},{9,8},{10,11... | collective-permute-start | bytes 1769480 | tf_op jit(solution)/shard_map/ppermute | solution.py:275
  14.3 1.7 %copy.22.refs_6_.refs_5_.refs_7_ = f32[8,384,2]{2,1,0:T(8,128)} copy(f32[8,384,2]{1,0,2:T(8,128)S(1)} %pad_maximum_fusion.1) | data formatting | bytes 49152 | tf_op jit(solution)/shard_map/stack | solution.py:295
  16.1 22.0 %collective-permute-done.4.refs_2_.refs_4_ = bf16[1,192,1536]{2,1,0:T(8,128)(2,1)} collective-permute-done((bf16[1,192,1536]{2,1,0:T(8,128)(2,1)}, bf16[1,192,1536]{2,1,0:T(8,128)(2,1)}, u32[]{:S(2)}, u32[]{:S(2)}) %collective-permute-start.4) | collective-permute-done | bytes 589856 | tf_op jit(solution)/shard_map/ppermute | solution.py:275
  38.2 0.6 collective-permute-start.5
  39.1 1.4 %copy-done = f32[8,384,2]{2,1,0:T(8,128)S(1)} copy-done((f32[8,384,2]{2,1,0:T(8,128)S(1)}, f32[8,384,2]{2,1,0:T(8,128)}, u32[]{:S(2)}) %copy-start) | copy-done | bytes 24600
  40.5 4.0 %pick.10 = (bf16[1,480,1536]{2,1,0:T(8,128)(2,1)}, bf16[1,480,1536]{2,1,0:T(8,128)(2,1)}) custom-call(s32[64]{0:T(128)S(1)} %copy-done.4, bf16[8,384,1536]{2,1,0:T(8,128)(2,1)} %refs_1_.13, bf16[384,1536]{1,0:T(8,128)(2,1)} %refs_2_.13, bf16[1,192,1536]{2,1,0:T(8,128)(2,1)S(1)} %collective-permute-done.3.refs_1_.refs_3_, ...), custom_call_target="tpu_custom_call" | custom-call | tf_op jit(solution)/shard_map/pick/pallas_call | solution.py:78
  44.5 0.6 collective-permute-start.10
  45.6 7.0 %collective-permute-done.5.refs_3_ = bf16[1,192,1536]{2,1,0:T(8,128)(2,1)} collective-permute-done((bf16[1,192,1536]{2,1,0:T(8,128)(2,1)}, bf16[1,192,1536]{2,1,0:T(8,128)(2,1)}, u32[]{:S(2)}, u32[]{:S(2)}) %collective-permute-start.5) | collective-permute-done | bytes 589856 | tf_op jit(solution)/shard_map/ppermute | solution.py:275
  52.6 9.1 %collective-permute-done.refs_3_.refs_0_ = bf16[1,768,1536]{2,1,0:T(8,128)(2,1)S(1)} collective-permute-done((bf16[1,768,1536]{2,1,0:T(8,128)(2,1)}, bf16[1,768,1536]{2,1,0:T(8,128)(2,1)S(1)}, u32[]{:S(2)}, u32[]{:S(2)}) %collective-permute-start) | collective-permute-done | bytes 2359328 | tf_op jit(solution)/shard_map/ppermute | solution.py:275
  61.8 1.3 %extract.2 = bf16[1,384,1536]{2,1,0:T(8,128)(2,1)} custom-call(bf16[1,768,1536]{2,1,0:T(8,128)(2,1)S(1)} %collective-permute-done.refs_3_.refs_0_), custom_call_target="tpu_custom_call" | custom-call | tf_op jit(solution)/shard_map/extract/pallas_call | solution.py:103
  63.0 0.8 copy-done.5
  64.4 1.8 %pick.11.refs_1_ = bf16[1,384,1536]{2,1,0:T(8,128)(2,1)S(1)} custom-call(s32[64]{0:T(128)S(1)} %copy-done.4, bf16[8,384,1536]{2,1,0:T(8,128)(2,1)} %refs_1_.13, bf16[384,1536]{1,0:T(8,128)(2,1)} %refs_2_.13, bf16[1,192,1536]{2,1,0:T(8,128)(2,1)S(1)} %collective-permute-done.3.refs_1_.refs_3_), custom_call_target="tpu_custom_call" | custom-call | tf_op jit(solution)/shard_map/pick/pallas_call | solution.py:78
  66.3 1.7 %collective-permute-done.9.refs_7_ = bf16[1,192,1536]{2,1,0:T(8,128)(2,1)} collective-permute-done((bf16[1,192,1536]{2,1,0:T(8,128)(2,1)}, bf16[1,192,1536]{2,1,0:T(8,128)(2,1)}, u32[]{:S(2)}, u32[]{:S(2)}) %collective-permute-start.9) | collective-permute-done | bytes 589856 | tf_op jit(solution)/shard_map/ppermute | solution.py:275
  68.0 2.9 %assemble.1 = bf16[4,2,192,1536]{3,2,1,0:T(8,128)(2,1)S(1)} custom-call(s32[2]{0:T(128)S(1)} %pad_add_fusion.place_ref, bf16[1,192,1536]{2,1,0:T(8,128)(2,1)} %get-tuple-element.27.refs_0_, bf16[1,192,1536]{2,1,0:T(8,128)(2,1)} %copy-done.2, bf16[1,192,1536]{2,1,0:T(8,128)(2,1)} %collective-permute-done.4.refs_2_.refs_4_, ...), custom_call_target="tpu_custom_call" | custom-call | tf_op jit(solution)/shard_map/assemble/pallas_call | solution.py:129
  70.9 2.0 %pick.13 = (bf16[1,192,1536]{2,1,0:T(8,128)(2,1)S(1)}, bf16[1,192,1536]{2,1,0:T(8,128)(2,1)S(1)}) custom-call(s32[64]{0:T(128)S(1)} %copy-done.4, bf16[8,384,1536]{2,1,0:T(8,128)(2,1)} %refs_1_.13, bf16[384,1536]{1,0:T(8,128)(2,1)} %refs_2_.13, bf16[1,768,1536]{2,1,0:T(8,128)(2,1)S(1)} %collective-permute-done.refs_3_.refs_0_), custom_call_target="tpu_custom_call" | custom-call | tf_op jit(solution)/shard_map/pick/pallas_call | solution.py:78
  72.9 2.0 %collective-permute-start.15 = (bf16[1,192,1536]{2,1,0:T(8,128)(2,1)S(1)}, bf16[1,192,1536]{2,1,0:T(8,128)(2,1)S(1)}, u32[]{:S(2)}, u32[]{:S(2)}) collective-permute-start(bf16[1,192,1536]{2,1,0:T(8,128)(2,1)S(1)} %get-tuple-element.36), channel_id=1, source_target_pairs={{0,12},{4,8},{8,4},{12,0},{16,28},{20,24},{24,20},{28,16},{1,13},{... | collective-permute-start | bytes 1769480 | tf_op jit(solution)/shard_map/ppermute | solution.py:275
  75.0 2.2 %pick.12 = (bf16[1,384,1536]{2,1,0:T(8,128)(2,1)S(1)}, bf16[1,384,1536]{2,1,0:T(8,128)(2,1)S(1)}) custom-call(s32[64]{0:T(128)S(1)} %copy-done.4, bf16[8,384,1536]{2,1,0:T(8,128)(2,1)} %refs_1_.13, bf16[384,1536]{1,0:T(8,128)(2,1)} %refs_2_.13, bf16[1,768,1536]{2,1,0:T(8,128)(2,1)S(1)} %collective-permute-done.refs_3_.refs_0_), custom_call_target="tpu_custom_call" | custom-call | tf_op jit(solution)/shard_map/pick/pallas_call | solution.py:78
  77.2 2.3 %pick.8 = (bf16[1,288,1536]{2,1,0:T(8,128)(2,1)S(1)}, bf16[1,288,1536]{2,1,0:T(8,128)(2,1)S(1)}, bf16[1,96,1536]{2,1,0:T(8,128)(2,1)S(1)}, bf16[1,96,1536]{2,1,0:T(8,128)(2,1)S(1)}) custom-call(s32[64]{0:T(128)S(1)} %copy-done.4, bf16[8,384,1536]{2,1,0:T(8,128)(2,1)} %refs_1_.13, bf16[384,1536]{1,0:T(8,128)(2,1)} %refs_2_.13, ...), custom_call_target="tpu_custom_call" | custom-call | tf_op jit(solution)/shard_map/pick/pallas_call | solution.py:78
  79.5 1.8 %pick.9 = (bf16[1,96,1536]{2,1,0:T(8,128)(2,1)S(1)}, bf16[1,96,1536]{2,1,0:T(8,128)(2,1)S(1)}) custom-call(s32[64]{0:T(128)S(1)} %copy-done.4, bf16[8,384,1536]{2,1,0:T(8,128)(2,1)} %refs_1_.13, bf16[384,1536]{1,0:T(8,128)(2,1)} %refs_2_.13, bf16[1,768,1536]{2,1,0:T(8,128)(2,1)S(1)} %collective-permute-done.refs_3_.refs_0_), custom_call_target="tpu_custom_call" | custom-call | tf_op jit(solution)/shard_map/pick/pallas_call | solution.py:78
  81.3 1.3 %collective-permute-start.16 = (bf16[1,192,1536]{2,1,0:T(8,128)(2,1)S(1)}, bf16[1,192,1536]{2,1,0:T(8,128)(2,1)S(1)}, u32[]{:S(2)}, u32[]{:S(2)}) collective-permute-start(bf16[1,192,1536]{2,1,0:T(8,128)(2,1)S(1)} %get-tuple-element.37), channel_id=1, source_target_pairs={{0,20},{4,16},{8,28},{12,24},{16,4},{20,0},{24,12},{28,8},{1,21},{... | collective-permute-start | bytes 1769480 | tf_op jit(solution)/shard_map/ppermute | solution.py:275
  82.6 12.3 %finish.1 = (bf16[8,384,1536]{2,1,0:T(8,128)(2,1)}, f32[8,128]{1,0:T(8,128)S(1)}) custom-call(s32[8]{0:T(128)S(1)} %select_reduce_fusion.2.refs_5_.slots_ref, bf16[8,384,1536]{2,1,0:T(8,128)(2,1)} %refs_1_.13, bf16[1,384,1536]{2,1,0:T(8,128)(2,1)S(1)} %pick.11.refs_1_, bf16[1,384,1536]{2,1,0:T(8,128)(2,1)} %collective-permute-done.12.refs_2_, ...), custom_call_target="tpu_custom_call" | custom-call | tf_op jit(solution)/shard_map/finish/pallas_call | solution.py:188
  94.9 1.1 extract.3
  97.0 6.6 %finish_together.3.refs_9_ = bf16[8,384,1536]{2,1,0:T(8,128)(2,1)} custom-call(s32[8]{0:T(128)S(1)} %select_reduce_fusion.2.refs_5_.slots_ref, bf16[1,384,1536]{2,1,0:T(8,128)(2,1)S(1)} %get-tuple-element.34.refs_5_.refs_0_, bf16[1,384,1536]{2,1,0:T(8,128)(2,1)S(1)} %get-tuple-element.35.refs_6_.refs_1_, ...), custom_call_target="tpu_custom_call", output_to_operand_aliasing={{}: (8, {})} | custom-call | tf_op jit(solution)/shard_map/finish_together/pallas_call | solution.py:245
  103.5 2.0 %collective-permute-done.15.refs_3_ = bf16[1,192,1536]{2,1,0:T(8,128)(2,1)S(1)} collective-permute-done((bf16[1,192,1536]{2,1,0:T(8,128)(2,1)S(1)}, bf16[1,192,1536]{2,1,0:T(8,128)(2,1)S(1)}, u32[]{:S(2)}, u32[]{:S(2)}) %collective-permute-start.15) | collective-permute-done | bytes 589856 | tf_op jit(solution)/shard_map/ppermute | solution.py:275
  105.6 4.3 %finish_together.4.refs_7_ = bf16[8,384,1536]{2,1,0:T(8,128)(2,1)} custom-call(s32[8]{0:T(128)S(1)} %select_reduce_fusion.2.refs_5_.slots_ref, bf16[1,288,1536]{2,1,0:T(8,128)(2,1)S(1)} %get-tuple-element.28.refs_7_.refs_0_, bf16[1,288,1536]{2,1,0:T(8,128)(2,1)S(1)} %get-tuple-element.29.refs_8_.refs_1_, ...), custom_call_target="tpu_custom_call", output_to_operand_aliasing={{}: (10, {})} | custom-call | tf_op jit(solution)/shard_map/finish_together/pallas_call | solution.py:245
  109.9 0.9 collective-permute-done.1.refs_2_
  110.7 0.6 collective-permute-done.2.refs_3_
  111.4 2.4 %finish_together.5 = bf16[8,384,1536]{2,1,0:T(8,128)(2,1)} custom-call(s32[8]{0:T(128)S(1)} %select_reduce_fusion.2.refs_5_.slots_ref, bf16[1,96,1536]{2,1,0:T(8,128)(2,1)S(1)} %get-tuple-element.23.refs_9_.refs_0_, bf16[1,96,1536]{2,1,0:T(8,128)(2,1)S(1)} %get-tuple-element.24.refs_10_.refs_1_, ...), custom_call_target="tpu_custom_call", output_to_operand_aliasing={{}: (8, {})} | custom-call | tf_op jit(solution)/shard_map/finish_together/pallas_call | solution.py:245
  (55 shorter events, 3.2 us)
Async XLA Ops:
  0.0 0.7 copy-start.3
  0.7 12.9 %copy-start.7 = (s32[8,24]{1,0:T(8,128)S(1)}, s32[8,24]{1,0:T(8,128)}, u32[]{:S(2)}) copy-start(s32[8,24]{1,0:T(8,128)} %param.12) | copy-start | bytes 2308
  0.7 13.1 %copy-start.9 = (s32[8,2]{0,1:T(2,128)S(1)}, s32[8,2]{0,1:T(2,128)}, u32[]{:S(2)}) copy-start(s32[8,2]{0,1:T(2,128)} %param.11) | copy-start | bytes 196
  0.7 13.1 %copy-start.8 = (f32[256]{0:T(256)S(1)}, f32[256]{0:T(256)}, u32[]{:S(2)}) copy-start(f32[256]{0:T(256)} %param.13) | copy-start | bytes 3076
  0.7 13.4 %copy-start.6 = (f32[1536]{0:T(1024)S(1)}, f32[1536]{0:T(1024)}, u32[]{:S(2)}) copy-start(f32[1536]{0:T(1024)} %param.14) | copy-start | bytes 18436
  5.4 10.6 %copy-start.4 = (s32[64]{0:T(128)S(1)}, s32[64]{0:T(128)}, u32[]{:S(2)}) copy-start(s32[64]{0:T(128)} %refs_0_.15) | copy-start | bytes 772
  5.4 10.6 %copy-start.10 = (s32[8]{0:T(128)S(1)}, s32[8]{0:T(128)}, u32[]{:S(2)}) copy-start(s32[8]{0:T(128)} %constant.48.clone) | copy-start | bytes 100
  5.5 56.3 %collective-permute-start = (bf16[1,768,1536]{2,1,0:T(8,128)(2,1)}, bf16[1,768,1536]{2,1,0:T(8,128)(2,1)S(1)}, u32[]{:S(2)}, u32[]{:S(2)}) collective-permute-start(bf16[1,768,1536]{2,1,0:T(8,128)(2,1)} %get-tuple-element.22), channel_id=1, source_target_pairs={{0,24},{4,28},{8,16},{12,20},{16,8},{20,12},{24,0},{28,4},{1,25},{... | collective-permute-start | bytes 7077896 | tf_op jit(solution)/shard_map/ppermute | solution.py:275
  9.4 28.7 %collective-permute-start.4 = (bf16[1,192,1536]{2,1,0:T(8,128)(2,1)}, bf16[1,192,1536]{2,1,0:T(8,128)(2,1)}, u32[]{:S(2)}, u32[]{:S(2)}) collective-permute-start(bf16[1,192,1536]{2,1,0:T(8,128)(2,1)} %get-tuple-element.27.refs_0_), channel_id=1, source_target_pairs={{0,2},{1,3},{2,0},{3,1},{4,6},{5,7},{6,4},{7,5},{8,10},{9,11},{10,... | collective-permute-start | bytes 1769480 | tf_op jit(solution)/shard_map/ppermute | solution.py:275
  12.0 26.7 %collective-permute-start.3 = (bf16[1,192,1536]{2,1,0:T(8,128)(2,1)}, bf16[1,192,1536]{2,1,0:T(8,128)(2,1)S(1)}, u32[]{:S(2)}, u32[]{:S(2)}) collective-permute-start(bf16[1,192,1536]{2,1,0:T(8,128)(2,1)} %get-tuple-element.27.refs_0_), channel_id=1, source_target_pairs={{0,1},{1,0},{2,3},{3,2},{4,5},{5,4},{6,7},{7,6},{8,9},{9,8},{10,11... | collective-permute-start | bytes 1769480 | tf_op jit(solution)/shard_map/ppermute | solution.py:275
  13.6 31.5 %collective-permute-start.6 = (bf16[1,192,1536]{2,1,0:T(8,128)(2,1)}, bf16[1,192,1536]{2,1,0:T(8,128)(2,1)}, u32[]{:S(2)}, u32[]{:S(2)}) collective-permute-start(bf16[1,192,1536]{2,1,0:T(8,128)(2,1)} %get-tuple-element.27.refs_0_), channel_id=1, source_target_pairs={{0,4},{4,0},{8,12},{12,8},{16,20},{20,16},{24,28},{28,24},{1,5},{5... | collective-permute-start | bytes 1769480 | tf_op jit(solution)/shard_map/ppermute | solution.py:275
  38.2 14.4 %collective-permute-start.5 = (bf16[1,192,1536]{2,1,0:T(8,128)(2,1)}, bf16[1,192,1536]{2,1,0:T(8,128)(2,1)}, u32[]{:S(2)}, u32[]{:S(2)}) collective-permute-start(bf16[1,192,1536]{2,1,0:T(8,128)(2,1)} %collective-permute-done.4.refs_2_.refs_4_), channel_id=1, source_target_pairs={{0,1},{1,0},{2,3},{3,2},{4,5},{5,4},{6,7},{7,6},{8,9},{9,8},{10,11... | collective-permute-start | bytes 1769480 | tf_op jit(solution)/shard_map/ppermute | solution.py:275
  38.7 25.7 %copy-start.2 = (bf16[1,192,1536]{2,1,0:T(8,128)(2,1)}, bf16[1,192,1536]{2,1,0:T(8,128)(2,1)S(1)}, u32[]{:S(2)}) copy-start(bf16[1,192,1536]{2,1,0:T(8,128)(2,1)S(1)} %collective-permute-done.3.refs_1_.refs_3_) | copy-start | bytes 1769476
  38.7 24.3 %collective-permute-start.7 = (bf16[1,192,1536]{2,1,0:T(8,128)(2,1)S(1)}, bf16[1,192,1536]{2,1,0:T(8,128)(2,1)S(1)}, u32[]{:S(2)}, u32[]{:S(2)}) collective-permute-start(bf16[1,192,1536]{2,1,0:T(8,128)(2,1)S(1)} %collective-permute-done.3.refs_1_.refs_3_), channel_id=1, source_target_pairs={{0,4},{4,0},{8,12},{12,8},{16,20},{20,16},{24,28},{28,24},{1,5},{5... | collective-permute-start | bytes 1769480 | tf_op jit(solution)/shard_map/ppermute | solution.py:275
  39.1 1.4 %copy-start = (f32[8,384,2]{2,1,0:T(8,128)S(1)}, f32[8,384,2]{2,1,0:T(8,128)}, u32[]{:S(2)}) copy-start(f32[8,384,2]{2,1,0:T(8,128)} %copy.22.refs_6_.refs_5_.refs_7_) | copy-start | bytes 73732
  44.5 50.4 %collective-permute-start.10 = (bf16[1,480,1536]{2,1,0:T(8,128)(2,1)}, bf16[1,480,1536]{2,1,0:T(8,128)(2,1)}, u32[]{:S(2)}, u32[]{:S(2)}) collective-permute-start(bf16[1,480,1536]{2,1,0:T(8,128)(2,1)} %get-tuple-element.30), channel_id=1, source_target_pairs={{0,8},{4,12},{8,0},{12,4},{16,24},{20,28},{24,16},{28,20},{1,9},{5... | collective-permute-start | bytes 4423688 | tf_op jit(solution)/shard_map/ppermute | solution.py:275
  45.1 49.8 %collective-permute-start.11 = (bf16[1,480,1536]{2,1,0:T(8,128)(2,1)}, bf16[1,480,1536]{2,1,0:T(8,128)(2,1)}, u32[]{:S(2)}, u32[]{:S(2)}) collective-permute-start(bf16[1,480,1536]{2,1,0:T(8,128)(2,1)} %get-tuple-element.31), channel_id=1, source_target_pairs={{0,16},{4,20},{8,24},{12,28},{16,0},{20,4},{24,8},{28,12},{1,17},{... | collective-permute-start | bytes 4423688 | tf_op jit(solution)/shard_map/ppermute | solution.py:275
  52.6 11.7 %collective-permute-start.8 = (bf16[1,192,1536]{2,1,0:T(8,128)(2,1)}, bf16[1,192,1536]{2,1,0:T(8,128)(2,1)}, u32[]{:S(2)}, u32[]{:S(2)}) collective-permute-start(bf16[1,192,1536]{2,1,0:T(8,128)(2,1)} %collective-permute-done.4.refs_2_.refs_4_), channel_id=1, source_target_pairs={{0,4},{4,0},{8,12},{12,8},{16,20},{20,16},{24,28},{28,24},{1,5},{5... | collective-permute-start | bytes 1769480 | tf_op jit(solution)/shard_map/ppermute | solution.py:275
  61.8 19.5 %collective-permute-start.12 = (bf16[1,384,1536]{2,1,0:T(8,128)(2,1)}, bf16[1,384,1536]{2,1,0:T(8,128)(2,1)}, u32[]{:S(2)}, u32[]{:S(2)}) collective-permute-start(bf16[1,384,1536]{2,1,0:T(8,128)(2,1)} %get-tuple-element.32), channel_id=1, source_target_pairs={{0,4},{4,0},{8,12},{12,8},{16,20},{20,16},{24,28},{28,24},{1,5},{5... | collective-permute-start | bytes 3538952 | tf_op jit(solution)/shard_map/ppermute | solution.py:275
  63.0 0.8 copy-start.5
  63.8 18.8 %collective-permute-start.13 = (bf16[1,384,1536]{2,1,0:T(8,128)(2,1)}, bf16[1,384,1536]{2,1,0:T(8,128)(2,1)}, u32[]{:S(2)}, u32[]{:S(2)}) collective-permute-start(bf16[1,384,1536]{2,1,0:T(8,128)(2,1)} %extract.2), channel_id=1, source_target_pairs={{0,4},{4,0},{8,12},{12,8},{16,20},{20,16},{24,28},{28,24},{1,5},{5... | collective-permute-start | bytes 3538952 | tf_op jit(solution)/shard_map/ppermute | solution.py:275
  64.4 3.7 %collective-permute-start.9 = (bf16[1,192,1536]{2,1,0:T(8,128)(2,1)}, bf16[1,192,1536]{2,1,0:T(8,128)(2,1)}, u32[]{:S(2)}, u32[]{:S(2)}) collective-permute-start(bf16[1,192,1536]{2,1,0:T(8,128)(2,1)} %collective-permute-done.5.refs_3_), channel_id=1, source_target_pairs={{0,4},{4,0},{8,12},{12,8},{16,20},{20,16},{24,28},{28,24},{1,5},{5... | collective-permute-start | bytes 1769480 | tf_op jit(solution)/shard_map/ppermute | solution.py:275
  72.9 32.6 %collective-permute-start.15 = (bf16[1,192,1536]{2,1,0:T(8,128)(2,1)S(1)}, bf16[1,192,1536]{2,1,0:T(8,128)(2,1)S(1)}, u32[]{:S(2)}, u32[]{:S(2)}) collective-permute-start(bf16[1,192,1536]{2,1,0:T(8,128)(2,1)S(1)} %get-tuple-element.36), channel_id=1, source_target_pairs={{0,12},{4,8},{8,4},{12,0},{16,28},{20,24},{24,20},{28,16},{1,13},{... | collective-permute-start | bytes 1769480 | tf_op jit(solution)/shard_map/ppermute | solution.py:275
  79.5 3.1 %copy-start.1 = (f32[8,384,2]{2,1,0:T(8,128)S(1)}, f32[8,384,2]{2,1,0:T(8,128)}, u32[]{:S(2)}) copy-start(f32[8,384,2]{2,1,0:T(8,128)} %copy.22.refs_6_.refs_5_.refs_7_) | copy-start | bytes 73732
  81.3 24.3 %collective-permute-start.16 = (bf16[1,192,1536]{2,1,0:T(8,128)(2,1)S(1)}, bf16[1,192,1536]{2,1,0:T(8,128)(2,1)S(1)}, u32[]{:S(2)}, u32[]{:S(2)}) collective-permute-start(bf16[1,192,1536]{2,1,0:T(8,128)(2,1)S(1)} %get-tuple-element.37), channel_id=1, source_target_pairs={{0,20},{4,16},{8,28},{12,24},{16,4},{20,0},{24,12},{28,8},{1,21},{... | collective-permute-start | bytes 1769480 | tf_op jit(solution)/shard_map/ppermute | solution.py:275
  96.0 9.6 %collective-permute-start.14 = (bf16[1,192,1536]{2,1,0:T(8,128)(2,1)S(1)}, bf16[1,192,1536]{2,1,0:T(8,128)(2,1)S(1)}, u32[]{:S(2)}, u32[]{:S(2)}) collective-permute-start(bf16[1,192,1536]{2,1,0:T(8,128)(2,1)S(1)} %extract.3), channel_id=1, source_target_pairs={{0,4},{4,0},{8,12},{12,8},{16,20},{20,16},{24,28},{28,24},{1,5},{5... | collective-permute-start | bytes 1769480 | tf_op jit(solution)/shard_map/ppermute | solution.py:275
  96.4 14.3 %collective-permute-start.1 = (bf16[1,96,1536]{2,1,0:T(8,128)(2,1)S(1)}, bf16[1,96,1536]{2,1,0:T(8,128)(2,1)S(1)}, u32[]{:S(2)}, u32[]{:S(2)}) collective-permute-start(bf16[1,96,1536]{2,1,0:T(8,128)(2,1)S(1)} %get-tuple-element.25.refs_3_), channel_id=1, source_target_pairs={{0,12},{4,8},{8,4},{12,0},{16,28},{20,24},{24,20},{28,16},{1,13},{... | collective-permute-start | bytes 884744 | tf_op jit(solution)/shard_map/ppermute | solution.py:275
  96.8 14.6 %collective-permute-start.2 = (bf16[1,96,1536]{2,1,0:T(8,128)(2,1)S(1)}, bf16[1,96,1536]{2,1,0:T(8,128)(2,1)S(1)}, u32[]{:S(2)}, u32[]{:S(2)}) collective-permute-start(bf16[1,96,1536]{2,1,0:T(8,128)(2,1)S(1)} %get-tuple-element.26.refs_4_), channel_id=1, source_target_pairs={{0,20},{4,16},{8,28},{12,24},{16,4},{20,0},{24,12},{28,8},{1,21},{... | collective-permute-start | bytes 884744 | tf_op jit(solution)/shard_map/ppermute | solution.py:275

commit v3 on v2

--- a/solution.py
+++ b/solution.py
@@ -32,11 +32,20 @@
         copy.wait()
 
 
-def pick_kernel(picks, core_rows, pair_dev, waits, *refs):
+def pick_kernel(picks, core_rows, pair_dev, waits, staged, *refs):
     mirror_ref, amps_ref, shard_ref = refs[:3]
-    outs, sems = refs[3 + waits:-1], refs[-1]
+    total = len(picks) + (core_rows > 0)
+    outs, stages = refs[3 + waits:3 + waits + total], refs[3 + waits + total:-2] if staged else None
+    sems, store_sems = refs[-2:]
     here = lax.axis_index("pair")
-    copies = []
+
+    def fetch(item, n):
+        source, out, part = item
+        return pltpu.make_async_copy(source, (stages if staged else outs)[out].at[0, part], sems.at[n])
+
+    def store(item, n):
+        _, out, part = item
+        return pltpu.make_async_copy(stages[out].at[0, part], outs[out].at[0, part], store_sems.at[n])
 
     def slot_of(peer, outgoing):
         found = jnp.int32(0)
@@ -52,35 +61,42 @@
             found = found + jnp.where(owner == (here if outgoing else peer), value, 0)
         return found
 
-    for (parts, outgoing), out in zip(picks, outs):
+    moves = []
+    for n, ((parts, outgoing), out) in enumerate(zip(picks, outs)):
         done = 0
         for peer, first, count in parts:
             slot = slot_of(peer(here), outgoing)
-            for at in range(0, count, count // PIECES):
-                size = count // PIECES
-                source = amps_ref.at[slot, pl.ds(first + at, size)]
-                copies.append(pltpu.make_async_copy(source, out.at[0, pl.ds(done + at, size)], sems.at[len(copies)]))
-                copies[-1].start()
+            size = count // PIECES if count % (16 * PIECES) == 0 else count
+            for at in range(0, count, size):
+                part = pl.ds(done + at, size)
+                moves.append((amps_ref.at[slot, pl.ds(first + at, size)], n, part))
+                fetch(moves[-1], len(moves) - 1).start()
             done += count
     if core_rows:
-        rows = pl.ds((here & 1) * core_rows, core_rows)
-        copies.append(pltpu.make_async_copy(shard_ref.at[rows], outs[-1].at[0], sems.at[len(copies)]))
-        copies[-1].start()
-    for copy in copies:
-        copy.wait()
-
-
-def pick(picks, mirror, amps, shard, core_rows=0, place=pltpu.VMEM, earlier=()):
+        rows = pl.ds(pl.multiple_of((here & 1) * core_rows, core_rows), core_rows)
+        moves.append((shard_ref.at[rows], len(outs) - 1, pl.ds(0, core_rows)))
+        fetch(moves[-1], len(moves) - 1).start()
+    for n, item in enumerate(moves):
+        fetch(item, n).wait()
+        if staged:
+            store(item, n).start()
+    if staged:
+        for n, item in enumerate(moves):
+            store(item, n).wait()
+
+
+def pick(picks, mirror, amps, shard, core_rows=0, earlier=(), staged=False):
     pair_dev, _, width = amps.shape
-    shapes = [place((1, sum(p[2] for p in parts), width), amps.dtype) for parts, _ in picks]
+    shapes = [jax.ShapeDtypeStruct((1, sum(p[2] for p in parts), width), amps.dtype) for parts, _ in picks]
     if core_rows:
-        shapes.append(place((1, core_rows, width), shard.dtype))
+        shapes.append(jax.ShapeDtypeStruct((1, core_rows, width), shard.dtype))
     return pl.pallas_call(
-        functools.partial(pick_kernel, picks, core_rows, pair_dev, len(earlier)),
+        functools.partial(pick_kernel, picks, core_rows, pair_dev, len(earlier), staged),
         out_shape=shapes,
         in_specs=[SMEM, HBM, HBM] + [ANY] * len(earlier),
-        out_specs=[WHOLE] * len(shapes),
-        scratch_shapes=[pltpu.SemaphoreType.DMA((PIECES * sum(len(parts) for parts, _ in picks) + 1,))],
+        out_specs=[ANY if staged else WHOLE] * len(shapes),
+        scratch_shapes=([pltpu.VMEM(shape.shape, shape.dtype) for shape in shapes] if staged else [])
+        + [pltpu.SemaphoreType.DMA((PIECES * sum(len(parts) for parts, _ in picks) + 1,))] * 2,
         compiler_params=pltpu.CompilerParams(vmem_limit_bytes=VMEM_BYTES),
         cost_estimate=FREE,
         name="pick",
@@ -307,9 +323,9 @@
         def peer(step):
             return lambda i: i ^ step
 
-        def take(parts, earlier=(), outgoing=True, core_rows=0, place=pltpu.VMEM):
+        def take(parts, earlier=(), outgoing=True, core_rows=0, staged=False):
             picks = [([(peer(step), first, count) for step, first, count in part], outgoing) for part in parts]
-            return pick(picks, mirror, amps, cycle_integrals, core_rows, place, earlier)
+            return pick(picks, mirror, amps, cycle_integrals, core_rows, earlier, staged)
 
         def shift(value, step):
             return move(value, "pair", peer(step))
@@ -320,7 +336,8 @@
         def quarters(step, first, count):
             return (step, first * quarter, count * quarter)
 
-        to_d, to1, rows0 = take([[whole(6), whole(7)], [whole(1)]], core_rows=core_rows)
+        to_d, = take([[whole(6), whole(7)]], staged=True)
+        to1, rows0 = take([[whole(1)]], [to_d], core_rows=core_rows, staged=True)
         from_d, from1 = shift(to_d, 6), swap_cores(to1)
         rows1, rows2 = move(rows0, "virt", lambda z: z ^ 1), move(rows0, "virt", lambda z: z ^ 2)
         rows3 = move(rows2, "virt", lambda z: z ^ 1)
@@ -328,7 +345,7 @@
         pieces += [swap_cores(piece) for piece in pieces]
         integrals = assemble(pieces, [0, 1, 2, 3] * 2, [1] * 4 + [0] * 4, place, planes)
         to_x, to_y = take(
-            [[whole(2), quarters(3, 0, 1)], [whole(4), quarters(5, 0, 1)]], [rows1, rows2, slots, down, across]
+            [[whole(2), quarters(3, 0, 1)], [whole(4), quarters(5, 0, 1)]], [rows1, rows2, slots, down, across], staged=True
         )
         from_x, from_y = shift(to_x, 2), shift(to_y, 4)
         to0, = take([[whole(0)]], [rows1])
@@ -357,7 +374,7 @@
         for k in range(pair_dev):
             offset = (1 + k * stride) % devices
             picks.append(([(lambda i, o=offset: lax.rem(i + devices - o, jnp.int32(devices)), 0, rows)], True))
-        *to_all, rows0 = pick(picks, mirror, amps, cycle_integrals, core_rows, pltpu.HBM)
+        *to_all, rows0 = pick(picks, mirror, amps, cycle_integrals, core_rows)
         mine = [rows0] + [move(rows0, "virt", lambda z, s=s: (z - s) % planes) for s in range(1, planes)]
         other = [swap_cores(piece) for piece in mine]
         integrals = assemble(

time: 114 us -> 113 us (level)
  waiting for transfers between devices: 43.5 us -> 41 us
    ppermute x17, waiting for transfers between devices: 43.5 us -> 41 us  [move(): return lax.ppermute(block, axis, [(i, to(i)) for i in range(n)])]
    pallas_call x7 -> x8, Pallas kernels: 18.9 us -> 19.7 us  [pick(): pl.pallas_call(functools.partial(pick_kernel, picks, core_rows, pair_dev,...]
  transfers between devices with their start and end apart: 17 -> 17, of which waited for: 7 -> 7; matrix products, arithmetic and copies ran while one was open for 2% -> 3% of each run, Pallas kernels for 37% -> 40%
where the time goes in v3:
time: 113 us; the launch traced here: 112 us
  Pallas kernels  50.5 us (45%)
  waiting for transfers between devices  41 us (36%)
  starting transfers between devices  14.5 us (13%)
  local copies, waits for them, and re-layouts  5.01 us (4%)
    ppermute x17, waiting for transfers between devices, move(): return lax.ppermute(block, axis, [(i, to(i)) for i in range(n)])  41 us
    pallas_call x8, Pallas kernels, pick(): pl.pallas_call(functools.partial(pick_kernel, picks, core_rows, pair_dev,...  19.7 us
    ppermute x17, starting transfers between devices, move(): return lax.ppermute(block, axis, [(i, to(i)) for i in range(n)])  14.5 us
    pallas_call x3, Pallas kernels, finish_together(): pl.pallas_call(functools.partial(finish_together_kernel, first, first_row...  13.2 us
    pallas_call x1, Pallas kernels, finish(): pl.pallas_call(functools.partial(finish_kernel, [[length for _, _, length...  12.3 us
    pallas_call x1, Pallas kernels, assemble(): pl.pallas_call(functools.partial(assemble_kernel, (firsts, sides), count)...  2.93 us
    unnamed x22, local copies, waits for them, and re-layouts  2.9 us
    pallas_call x2, Pallas kernels, extract(): pl.pallas_call(functools.partial(extract_kernel, [part[1:] for part in pa...  2.33 us
  transfers between devices with their start and end apart: 17, of which 7 were waited for; matrix products, arithmetic and copies ran while one was open for 3% of the time, Pallas kernels for 40%

profile of v3, /device:TPU:0, one launch (start us, length us, event | category | flops | bytes accessed | tf_op | source)
XLA Modules:
  0.0 112.1 jit_solution(3757804351728978262)
XLA Ops:
  0.0 0.7 copy-done.3
  0.7 3.1 %pick.8.refs_3_ = bf16[1,768,1536]{2,1,0:T(8,128)(2,1)} custom-call(s32[64]{0:T(128)S(1)} %copy-done.3, bf16[8,384,1536]{2,1,0:T(8,128)(2,1)} %refs_1_.15, bf16[384,1536]{1,0:T(8,128)(2,1)} %refs_2_.15), custom_call_target="tpu_custom_call" | custom-call | tf_op jit(solution)/shard_map/pick/pallas_call | solution.py:93
  3.8 4.0 %collective-permute-start = (bf16[1,768,1536]{2,1,0:T(8,128)(2,1)}, bf16[1,768,1536]{2,1,0:T(8,128)(2,1)S(1)}, u32[]{:S(2)}, u32[]{:S(2)}) collective-permute-start(bf16[1,768,1536]{2,1,0:T(8,128)(2,1)} %pick.8.refs_3_), channel_id=1, source_target_pairs={{0,24},{4,28},{8,16},{12,20},{16,8},{20,12},{24,0},{28,4},{1,25},{... | collective-permute-start | bytes 7077896 | tf_op jit(solution)/shard_map/ppermute | solution.py:291
  7.7 2.9 %pick.11 = (bf16[1,384,1536]{2,1,0:T(8,128)(2,1)}, bf16[1,192,1536]{2,1,0:T(8,128)(2,1)}) custom-call(s32[64]{0:T(128)S(1)} %copy-done.3, bf16[8,384,1536]{2,1,0:T(8,128)(2,1)} %refs_1_.15, bf16[384,1536]{1,0:T(8,128)(2,1)} %refs_2_.15, bf16[1,768,1536]{2,1,0:T(8,128)(2,1)} %pick.8.refs_3_), custom_call_target="tpu_custom_call" | custom-call | tf_op jit(solution)/shard_map/pick/pallas_call | solution.py:93
  10.7 2.7 %collective-permute-start.4 = (bf16[1,192,1536]{2,1,0:T(8,128)(2,1)}, bf16[1,192,1536]{2,1,0:T(8,128)(2,1)}, u32[]{:S(2)}, u32[]{:S(2)}) collective-permute-start(bf16[1,192,1536]{2,1,0:T(8,128)(2,1)} %get-tuple-element.25.refs_0_), channel_id=1, source_target_pairs={{0,2},{1,3},{2,0},{3,1},{4,6},{5,7},{6,4},{7,5},{8,10},{9,11},{10,... | collective-permute-start | bytes 1769480 | tf_op jit(solution)/shard_map/ppermute | solution.py:291
  13.3 1.6 %collective-permute-start.3 = (bf16[1,192,1536]{2,1,0:T(8,128)(2,1)}, bf16[1,192,1536]{2,1,0:T(8,128)(2,1)S(1)}, u32[]{:S(2)}, u32[]{:S(2)}) collective-permute-start(bf16[1,192,1536]{2,1,0:T(8,128)(2,1)} %get-tuple-element.25.refs_0_), channel_id=1, source_target_pairs={{0,1},{1,0},{2,3},{3,2},{4,5},{5,4},{6,7},{7,6},{8,9},{9,8},{10,11... | collective-permute-start | bytes 1769480 | tf_op jit(solution)/shard_map/ppermute | solution.py:291
  15.6 1.7 %copy.22.refs_6_.refs_5_.refs_7_ = f32[8,384,2]{2,1,0:T(8,128)} copy(f32[8,384,2]{1,0,2:T(8,128)S(1)} %pad_maximum_fusion.1) | data formatting | bytes 49152 | tf_op jit(solution)/shard_map/stack | solution.py:311
  17.4 22.0 %collective-permute-done.4.refs_2_.refs_4_ = bf16[1,192,1536]{2,1,0:T(8,128)(2,1)} collective-permute-done((bf16[1,192,1536]{2,1,0:T(8,128)(2,1)}, bf16[1,192,1536]{2,1,0:T(8,128)(2,1)}, u32[]{:S(2)}, u32[]{:S(2)}) %collective-permute-start.4) | collective-permute-done | bytes 589856 | tf_op jit(solution)/shard_map/ppermute | solution.py:291
  40.4 1.4 %copy-done = f32[8,384,2]{2,1,0:T(8,128)S(1)} copy-done((f32[8,384,2]{2,1,0:T(8,128)S(1)}, f32[8,384,2]{2,1,0:T(8,128)}, u32[]{:S(2)}) %copy-start) | copy-done | bytes 24600
  41.8 3.4 %pick.12 = (bf16[1,480,1536]{2,1,0:T(8,128)(2,1)}, bf16[1,480,1536]{2,1,0:T(8,128)(2,1)}) custom-call(s32[64]{0:T(128)S(1)} %copy-done.4, bf16[8,384,1536]{2,1,0:T(8,128)(2,1)} %refs_1_.15, bf16[384,1536]{1,0:T(8,128)(2,1)} %refs_2_.15, bf16[1,192,1536]{2,1,0:T(8,128)(2,1)S(1)} %collective-permute-done.3.refs_1_.refs_3_, ...), custom_call_target="tpu_custom_call" | custom-call | tf_op jit(solution)/shard_map/pick/pallas_call | solution.py:93
  45.2 0.6 collective-permute-start.10
  46.3 7.6 %collective-permute-done.5.refs_3_ = bf16[1,192,1536]{2,1,0:T(8,128)(2,1)} collective-permute-done((bf16[1,192,1536]{2,1,0:T(8,128)(2,1)}, bf16[1,192,1536]{2,1,0:T(8,128)(2,1)}, u32[]{:S(2)}, u32[]{:S(2)}) %collective-permute-start.5) | collective-permute-done | bytes 589856 | tf_op jit(solution)/shard_map/ppermute | solution.py:291
  53.9 6.2 %collective-permute-done.refs_3_.refs_0_ = bf16[1,768,1536]{2,1,0:T(8,128)(2,1)S(1)} collective-permute-done((bf16[1,768,1536]{2,1,0:T(8,128)(2,1)}, bf16[1,768,1536]{2,1,0:T(8,128)(2,1)S(1)}, u32[]{:S(2)}, u32[]{:S(2)}) %collective-permute-start) | collective-permute-done | bytes 2359328 | tf_op jit(solution)/shard_map/ppermute | solution.py:291
  60.1 1.3 %extract.2 = bf16[1,384,1536]{2,1,0:T(8,128)(2,1)} custom-call(bf16[1,768,1536]{2,1,0:T(8,128)(2,1)S(1)} %collective-permute-done.refs_3_.refs_0_), custom_call_target="tpu_custom_call" | custom-call | tf_op jit(solution)/shard_map/extract/pallas_call | solution.py:119
  61.4 0.8 copy-done.5
  62.8 1.9 %pick.13.refs_1_ = bf16[1,384,1536]{2,1,0:T(8,128)(2,1)S(1)} custom-call(s32[64]{0:T(128)S(1)} %copy-done.4, bf16[8,384,1536]{2,1,0:T(8,128)(2,1)} %refs_1_.15, bf16[384,1536]{1,0:T(8,128)(2,1)} %refs_2_.15, bf16[1,192,1536]{2,1,0:T(8,128)(2,1)S(1)} %collective-permute-done.3.refs_1_.refs_3_), custom_call_target="tpu_custom_call" | custom-call | tf_op jit(solution)/shard_map/pick/pallas_call | solution.py:93
  64.6 1.7 %collective-permute-done.9.refs_7_ = bf16[1,192,1536]{2,1,0:T(8,128)(2,1)} collective-permute-done((bf16[1,192,1536]{2,1,0:T(8,128)(2,1)}, bf16[1,192,1536]{2,1,0:T(8,128)(2,1)}, u32[]{:S(2)}, u32[]{:S(2)}) %collective-permute-start.9) | collective-permute-done | bytes 589856 | tf_op jit(solution)/shard_map/ppermute | solution.py:291
  66.3 2.9 %assemble.1 = bf16[4,2,192,1536]{3,2,1,0:T(8,128)(2,1)S(1)} custom-call(s32[2]{0:T(128)S(1)} %pad_add_fusion.place_ref, bf16[1,192,1536]{2,1,0:T(8,128)(2,1)} %get-tuple-element.25.refs_0_, bf16[1,192,1536]{2,1,0:T(8,128)(2,1)} %copy-done.2, bf16[1,192,1536]{2,1,0:T(8,128)(2,1)} %collective-permute-done.4.refs_2_.refs_4_, ...), custom_call_target="tpu_custom_call" | custom-call | tf_op jit(solution)/shard_map/assemble/pallas_call | solution.py:145
  69.3 2.0 %pick.15 = (bf16[1,192,1536]{2,1,0:T(8,128)(2,1)S(1)}, bf16[1,192,1536]{2,1,0:T(8,128)(2,1)S(1)}) custom-call(s32[64]{0:T(128)S(1)} %copy-done.4, bf16[8,384,1536]{2,1,0:T(8,128)(2,1)} %refs_1_.15, bf16[384,1536]{1,0:T(8,128)(2,1)} %refs_2_.15, bf16[1,768,1536]{2,1,0:T(8,128)(2,1)S(1)} %collective-permute-done.refs_3_.refs_0_), custom_call_target="tpu_custom_call" | custom-call | tf_op jit(solution)/shard_map/pick/pallas_call | solution.py:93
  71.3 2.0 %collective-permute-start.15 = (bf16[1,192,1536]{2,1,0:T(8,128)(2,1)S(1)}, bf16[1,192,1536]{2,1,0:T(8,128)(2,1)S(1)}, u32[]{:S(2)}, u32[]{:S(2)}) collective-permute-start(bf16[1,192,1536]{2,1,0:T(8,128)(2,1)S(1)} %get-tuple-element.34), channel_id=1, source_target_pairs={{0,12},{4,8},{8,4},{12,0},{16,28},{20,24},{24,20},{28,16},{1,13},{... | collective-permute-start | bytes 1769480 | tf_op jit(solution)/shard_map/ppermute | solution.py:291
  73.4 2.3 %pick.14 = (bf16[1,384,1536]{2,1,0:T(8,128)(2,1)S(1)}, bf16[1,384,1536]{2,1,0:T(8,128)(2,1)S(1)}) custom-call(s32[64]{0:T(128)S(1)} %copy-done.4, bf16[8,384,1536]{2,1,0:T(8,128)(2,1)} %refs_1_.15, bf16[384,1536]{1,0:T(8,128)(2,1)} %refs_2_.15, bf16[1,768,1536]{2,1,0:T(8,128)(2,1)S(1)} %collective-permute-done.refs_3_.refs_0_), custom_call_target="tpu_custom_call" | custom-call | tf_op jit(solution)/shard_map/pick/pallas_call | solution.py:93
  75.6 2.4 %pick.9 = (bf16[1,288,1536]{2,1,0:T(8,128)(2,1)S(1)}, bf16[1,288,1536]{2,1,0:T(8,128)(2,1)S(1)}, bf16[1,96,1536]{2,1,0:T(8,128)(2,1)S(1)}, bf16[1,96,1536]{2,1,0:T(8,128)(2,1)S(1)}) custom-call(s32[64]{0:T(128)S(1)} %copy-done.4, bf16[8,384,1536]{2,1,0:T(8,128)(2,1)} %refs_1_.15, bf16[384,1536]{1,0:T(8,128)(2,1)} %refs_2_.15, ...), custom_call_target="tpu_custom_call" | custom-call | tf_op jit(solution)/shard_map/pick/pallas_call | solution.py:93
  78.0 1.8 %pick.10 = (bf16[1,96,1536]{2,1,0:T(8,128)(2,1)S(1)}, bf16[1,96,1536]{2,1,0:T(8,128)(2,1)S(1)}) custom-call(s32[64]{0:T(128)S(1)} %copy-done.4, bf16[8,384,1536]{2,1,0:T(8,128)(2,1)} %refs_1_.15, bf16[384,1536]{1,0:T(8,128)(2,1)} %refs_2_.15, bf16[1,768,1536]{2,1,0:T(8,128)(2,1)S(1)} %collective-permute-done.refs_3_.refs_0_), custom_call_target="tpu_custom_call" | custom-call | tf_op jit(solution)/shard_map/pick/pallas_call | solution.py:93
  79.9 1.3 %collective-permute-start.16 = (bf16[1,192,1536]{2,1,0:T(8,128)(2,1)S(1)}, bf16[1,192,1536]{2,1,0:T(8,128)(2,1)S(1)}, u32[]{:S(2)}, u32[]{:S(2)}) collective-permute-start(bf16[1,192,1536]{2,1,0:T(8,128)(2,1)S(1)} %get-tuple-element.35), channel_id=1, source_target_pairs={{0,20},{4,16},{8,28},{12,24},{16,4},{20,0},{24,12},{28,8},{1,21},{... | collective-permute-start | bytes 1769480 | tf_op jit(solution)/shard_map/ppermute | solution.py:291
  81.2 12.3 %finish.1 = (bf16[8,384,1536]{2,1,0:T(8,128)(2,1)}, f32[8,128]{1,0:T(8,128)S(1)}) custom-call(s32[8]{0:T(128)S(1)} %select_reduce_fusion.2.refs_5_.slots_ref, bf16[8,384,1536]{2,1,0:T(8,128)(2,1)} %refs_1_.15, bf16[1,384,1536]{2,1,0:T(8,128)(2,1)S(1)} %pick.13.refs_1_, bf16[1,384,1536]{2,1,0:T(8,128)(2,1)} %collective-permute-done.12.refs_2_, ...), custom_call_target="tpu_custom_call" | custom-call | tf_op jit(solution)/shard_map/finish/pallas_call | solution.py:204
  93.5 1.1 extract.3
  95.4 6.6 %finish_together.3.refs_9_ = bf16[8,384,1536]{2,1,0:T(8,128)(2,1)} custom-call(s32[8]{0:T(128)S(1)} %select_reduce_fusion.2.refs_5_.slots_ref, bf16[1,384,1536]{2,1,0:T(8,128)(2,1)S(1)} %get-tuple-element.32.refs_5_.refs_0_, bf16[1,384,1536]{2,1,0:T(8,128)(2,1)S(1)} %get-tuple-element.33.refs_6_.refs_1_, ...), custom_call_target="tpu_custom_call", output_to_operand_aliasing={{}: (8, {})} | custom-call | tf_op jit(solution)/shard_map/finish_together/pallas_call | solution.py:261
  101.9 2.0 %collective-permute-done.15.refs_3_ = bf16[1,192,1536]{2,1,0:T(8,128)(2,1)S(1)} collective-permute-done((bf16[1,192,1536]{2,1,0:T(8,128)(2,1)S(1)}, bf16[1,192,1536]{2,1,0:T(8,128)(2,1)S(1)}, u32[]{:S(2)}, u32[]{:S(2)}) %collective-permute-start.15) | collective-permute-done | bytes 589856 | tf_op jit(solution)/shard_map/ppermute | solution.py:291
  103.9 4.3 %finish_together.4.refs_7_ = bf16[8,384,1536]{2,1,0:T(8,128)(2,1)} custom-call(s32[8]{0:T(128)S(1)} %select_reduce_fusion.2.refs_5_.slots_ref, bf16[1,288,1536]{2,1,0:T(8,128)(2,1)S(1)} %get-tuple-element.26.refs_7_.refs_0_, bf16[1,288,1536]{2,1,0:T(8,128)(2,1)S(1)} %get-tuple-element.27.refs_8_.refs_1_, ...), custom_call_target="tpu_custom_call", output_to_operand_aliasing={{}: (10, {})} | custom-call | tf_op jit(solution)/shard_map/finish_together/pallas_call | solution.py:261
  108.2 0.9 collective-permute-done.1.refs_2_
  109.1 0.6 collective-permute-done.2.refs_3_
  109.7 2.4 %finish_together.5 = bf16[8,384,1536]{2,1,0:T(8,128)(2,1)} custom-call(s32[8]{0:T(128)S(1)} %select_reduce_fusion.2.refs_5_.slots_ref, bf16[1,96,1536]{2,1,0:T(8,128)(2,1)S(1)} %get-tuple-element.21.refs_9_.refs_0_, bf16[1,96,1536]{2,1,0:T(8,128)(2,1)S(1)} %get-tuple-element.22.refs_10_.refs_1_, ...), custom_call_target="tpu_custom_call", output_to_operand_aliasing={{}: (8, {})} | custom-call | tf_op jit(solution)/shard_map/finish_together/pallas_call | solution.py:261
  (56 shorter events, 3.6 us)
Async XLA Ops:
  0.0 0.7 copy-start.3
  3.7 11.2 %copy-start.7 = (s32[8,24]{1,0:T(8,128)S(1)}, s32[8,24]{1,0:T(8,128)}, u32[]{:S(2)}) copy-start(s32[8,24]{1,0:T(8,128)} %param.12) | copy-start | bytes 2308
  3.8 11.3 %copy-start.9 = (s32[8,2]{0,1:T(2,128)S(1)}, s32[8,2]{0,1:T(2,128)}, u32[]{:S(2)}) copy-start(s32[8,2]{0,1:T(2,128)} %param.11) | copy-start | bytes 196
  3.8 11.3 %copy-start.8 = (f32[256]{0:T(256)S(1)}, f32[256]{0:T(256)}, u32[]{:S(2)}) copy-start(f32[256]{0:T(256)} %param.13) | copy-start | bytes 3076
  3.8 11.6 %copy-start.6 = (f32[1536]{0:T(1024)S(1)}, f32[1536]{0:T(1024)}, u32[]{:S(2)}) copy-start(f32[1536]{0:T(1024)} %param.14) | copy-start | bytes 18436
  3.8 56.3 %collective-permute-start = (bf16[1,768,1536]{2,1,0:T(8,128)(2,1)}, bf16[1,768,1536]{2,1,0:T(8,128)(2,1)S(1)}, u32[]{:S(2)}, u32[]{:S(2)}) collective-permute-start(bf16[1,768,1536]{2,1,0:T(8,128)(2,1)} %pick.8.refs_3_), channel_id=1, source_target_pairs={{0,24},{4,28},{8,16},{12,20},{16,8},{20,12},{24,0},{28,4},{1,25},{... | collective-permute-start | bytes 7077896 | tf_op jit(solution)/shard_map/ppermute | solution.py:291
  10.6 6.7 %copy-start.4 = (s32[64]{0:T(128)S(1)}, s32[64]{0:T(128)}, u32[]{:S(2)}) copy-start(s32[64]{0:T(128)} %refs_0_.17) | copy-start | bytes 772
  10.6 6.7 %copy-start.10 = (s32[8]{0:T(128)S(1)}, s32[8]{0:T(128)}, u32[]{:S(2)}) copy-start(s32[8]{0:T(128)} %constant.48.clone) | copy-start | bytes 100
  10.7 28.8 %collective-permute-start.4 = (bf16[1,192,1536]{2,1,0:T(8,128)(2,1)}, bf16[1,192,1536]{2,1,0:T(8,128)(2,1)}, u32[]{:S(2)}, u32[]{:S(2)}) collective-permute-start(bf16[1,192,1536]{2,1,0:T(8,128)(2,1)} %get-tuple-element.25.refs_0_), channel_id=1, source_target_pairs={{0,2},{1,3},{2,0},{3,1},{4,6},{5,7},{6,4},{7,5},{8,10},{9,11},{10,... | collective-permute-start | bytes 1769480 | tf_op jit(solution)/shard_map/ppermute | solution.py:291
  13.3 26.7 %collective-permute-start.3 = (bf16[1,192,1536]{2,1,0:T(8,128)(2,1)}, bf16[1,192,1536]{2,1,0:T(8,128)(2,1)S(1)}, u32[]{:S(2)}, u32[]{:S(2)}) collective-permute-start(bf16[1,192,1536]{2,1,0:T(8,128)(2,1)} %get-tuple-element.25.refs_0_), channel_id=1, source_target_pairs={{0,1},{1,0},{2,3},{3,2},{4,5},{5,4},{6,7},{7,6},{8,9},{9,8},{10,11... | collective-permute-start | bytes 1769480 | tf_op jit(solution)/shard_map/ppermute | solution.py:291
  14.9 30.9 %collective-permute-start.6 = (bf16[1,192,1536]{2,1,0:T(8,128)(2,1)}, bf16[1,192,1536]{2,1,0:T(8,128)(2,1)}, u32[]{:S(2)}, u32[]{:S(2)}) collective-permute-start(bf16[1,192,1536]{2,1,0:T(8,128)(2,1)} %get-tuple-element.25.refs_0_), channel_id=1, source_target_pairs={{0,4},{4,0},{8,12},{12,8},{16,20},{20,16},{24,28},{28,24},{1,5},{5... | collective-permute-start | bytes 1769480 | tf_op jit(solution)/shard_map/ppermute | solution.py:291
  39.5 14.4 %collective-permute-start.5 = (bf16[1,192,1536]{2,1,0:T(8,128)(2,1)}, bf16[1,192,1536]{2,1,0:T(8,128)(2,1)}, u32[]{:S(2)}, u32[]{:S(2)}) collective-permute-start(bf16[1,192,1536]{2,1,0:T(8,128)(2,1)} %collective-permute-done.4.refs_2_.refs_4_), channel_id=1, source_target_pairs={{0,1},{1,0},{2,3},{3,2},{4,5},{5,4},{6,7},{7,6},{8,9},{9,8},{10,11... | collective-permute-start | bytes 1769480 | tf_op jit(solution)/shard_map/ppermute | solution.py:291
  40.0 22.7 %copy-start.2 = (bf16[1,192,1536]{2,1,0:T(8,128)(2,1)}, bf16[1,192,1536]{2,1,0:T(8,128)(2,1)S(1)}, u32[]{:S(2)}) copy-start(bf16[1,192,1536]{2,1,0:T(8,128)(2,1)S(1)} %collective-permute-done.3.refs_1_.refs_3_) | copy-start | bytes 1769476
  40.0 21.3 %collective-permute-start.7 = (bf16[1,192,1536]{2,1,0:T(8,128)(2,1)S(1)}, bf16[1,192,1536]{2,1,0:T(8,128)(2,1)S(1)}, u32[]{:S(2)}, u32[]{:S(2)}) collective-permute-start(bf16[1,192,1536]{2,1,0:T(8,128)(2,1)S(1)} %collective-permute-done.3.refs_1_.refs_3_), channel_id=1, source_target_pairs={{0,4},{4,0},{8,12},{12,8},{16,20},{20,16},{24,28},{28,24},{1,5},{5... | collective-permute-start | bytes 1769480 | tf_op jit(solution)/shard_map/ppermute | solution.py:291
  40.4 1.4 %copy-start = (f32[8,384,2]{2,1,0:T(8,128)S(1)}, f32[8,384,2]{2,1,0:T(8,128)}, u32[]{:S(2)}) copy-start(f32[8,384,2]{2,1,0:T(8,128)} %copy.22.refs_6_.refs_5_.refs_7_) | copy-start | bytes 73732
  45.2 48.3 %collective-permute-start.10 = (bf16[1,480,1536]{2,1,0:T(8,128)(2,1)}, bf16[1,480,1536]{2,1,0:T(8,128)(2,1)}, u32[]{:S(2)}, u32[]{:S(2)}) collective-permute-start(bf16[1,480,1536]{2,1,0:T(8,128)(2,1)} %get-tuple-element.28), channel_id=1, source_target_pairs={{0,8},{4,12},{8,0},{12,4},{16,24},{20,28},{24,16},{28,20},{1,9},{5... | collective-permute-start | bytes 4423688 | tf_op jit(solution)/shard_map/ppermute | solution.py:291
  45.8 47.7 %collective-permute-start.11 = (bf16[1,480,1536]{2,1,0:T(8,128)(2,1)}, bf16[1,480,1536]{2,1,0:T(8,128)(2,1)}, u32[]{:S(2)}, u32[]{:S(2)}) collective-permute-start(bf16[1,480,1536]{2,1,0:T(8,128)(2,1)} %get-tuple-element.29), channel_id=1, source_target_pairs={{0,16},{4,20},{8,24},{12,28},{16,0},{20,4},{24,8},{28,12},{1,17},{... | collective-permute-start | bytes 4423688 | tf_op jit(solution)/shard_map/ppermute | solution.py:291
  53.9 8.8 %collective-permute-start.8 = (bf16[1,192,1536]{2,1,0:T(8,128)(2,1)}, bf16[1,192,1536]{2,1,0:T(8,128)(2,1)}, u32[]{:S(2)}, u32[]{:S(2)}) collective-permute-start(bf16[1,192,1536]{2,1,0:T(8,128)(2,1)} %collective-permute-done.4.refs_2_.refs_4_), channel_id=1, source_target_pairs={{0,4},{4,0},{8,12},{12,8},{16,20},{20,16},{24,28},{28,24},{1,5},{5... | collective-permute-start | bytes 1769480 | tf_op jit(solution)/shard_map/ppermute | solution.py:291
  60.1 19.8 %collective-permute-start.12 = (bf16[1,384,1536]{2,1,0:T(8,128)(2,1)}, bf16[1,384,1536]{2,1,0:T(8,128)(2,1)}, u32[]{:S(2)}, u32[]{:S(2)}) collective-permute-start(bf16[1,384,1536]{2,1,0:T(8,128)(2,1)} %get-tuple-element.30), channel_id=1, source_target_pairs={{0,4},{4,0},{8,12},{12,8},{16,20},{20,16},{24,28},{28,24},{1,5},{5... | collective-permute-start | bytes 3538952 | tf_op jit(solution)/shard_map/ppermute | solution.py:291
  61.4 0.8 copy-start.5
  62.2 19.1 %collective-permute-start.13 = (bf16[1,384,1536]{2,1,0:T(8,128)(2,1)}, bf16[1,384,1536]{2,1,0:T(8,128)(2,1)}, u32[]{:S(2)}, u32[]{:S(2)}) collective-permute-start(bf16[1,384,1536]{2,1,0:T(8,128)(2,1)} %extract.2), channel_id=1, source_target_pairs={{0,4},{4,0},{8,12},{12,8},{16,20},{20,16},{24,28},{28,24},{1,5},{5... | collective-permute-start | bytes 3538952 | tf_op jit(solution)/shard_map/ppermute | solution.py:291
  62.7 3.7 %collective-permute-start.9 = (bf16[1,192,1536]{2,1,0:T(8,128)(2,1)}, bf16[1,192,1536]{2,1,0:T(8,128)(2,1)}, u32[]{:S(2)}, u32[]{:S(2)}) collective-permute-start(bf16[1,192,1536]{2,1,0:T(8,128)(2,1)} %collective-permute-done.5.refs_3_), channel_id=1, source_target_pairs={{0,4},{4,0},{8,12},{12,8},{16,20},{20,16},{24,28},{28,24},{1,5},{5... | collective-permute-start | bytes 1769480 | tf_op jit(solution)/shard_map/ppermute | solution.py:291
  71.3 32.6 %collective-permute-start.15 = (bf16[1,192,1536]{2,1,0:T(8,128)(2,1)S(1)}, bf16[1,192,1536]{2,1,0:T(8,128)(2,1)S(1)}, u32[]{:S(2)}, u32[]{:S(2)}) collective-permute-start(bf16[1,192,1536]{2,1,0:T(8,128)(2,1)S(1)} %get-tuple-element.34), channel_id=1, source_target_pairs={{0,12},{4,8},{8,4},{12,0},{16,28},{20,24},{24,20},{28,16},{1,13},{... | collective-permute-start | bytes 1769480 | tf_op jit(solution)/shard_map/ppermute | solution.py:291
  78.0 3.2 %copy-start.1 = (f32[8,384,2]{2,1,0:T(8,128)S(1)}, f32[8,384,2]{2,1,0:T(8,128)}, u32[]{:S(2)}) copy-start(f32[8,384,2]{2,1,0:T(8,128)} %copy.22.refs_6_.refs_5_.refs_7_) | copy-start | bytes 73732
  79.9 24.0 %collective-permute-start.16 = (bf16[1,192,1536]{2,1,0:T(8,128)(2,1)S(1)}, bf16[1,192,1536]{2,1,0:T(8,128)(2,1)S(1)}, u32[]{:S(2)}, u32[]{:S(2)}) collective-permute-start(bf16[1,192,1536]{2,1,0:T(8,128)(2,1)S(1)} %get-tuple-element.35), channel_id=1, source_target_pairs={{0,20},{4,16},{8,28},{12,24},{16,4},{20,0},{24,12},{28,8},{1,21},{... | collective-permute-start | bytes 1769480 | tf_op jit(solution)/shard_map/ppermute | solution.py:291
  94.6 9.3 %collective-permute-start.14 = (bf16[1,192,1536]{2,1,0:T(8,128)(2,1)S(1)}, bf16[1,192,1536]{2,1,0:T(8,128)(2,1)S(1)}, u32[]{:S(2)}, u32[]{:S(2)}) collective-permute-start(bf16[1,192,1536]{2,1,0:T(8,128)(2,1)S(1)} %extract.3), channel_id=1, source_target_pairs={{0,4},{4,0},{8,12},{12,8},{16,20},{20,16},{24,28},{28,24},{1,5},{5... | collective-permute-start | bytes 1769480 | tf_op jit(solution)/shard_map/ppermute | solution.py:291
  95.0 14.0 %collective-permute-start.1 = (bf16[1,96,1536]{2,1,0:T(8,128)(2,1)S(1)}, bf16[1,96,1536]{2,1,0:T(8,128)(2,1)S(1)}, u32[]{:S(2)}, u32[]{:S(2)}) collective-permute-start(bf16[1,96,1536]{2,1,0:T(8,128)(2,1)S(1)} %get-tuple-element.23.refs_3_), channel_id=1, source_target_pairs={{0,12},{4,8},{8,4},{12,0},{16,28},{20,24},{24,20},{28,16},{1,13},{... | collective-permute-start | bytes 884744 | tf_op jit(solution)/shard_map/ppermute | solution.py:291
  95.3 14.4 %collective-permute-start.2 = (bf16[1,96,1536]{2,1,0:T(8,128)(2,1)S(1)}, bf16[1,96,1536]{2,1,0:T(8,128)(2,1)S(1)}, u32[]{:S(2)}, u32[]{:S(2)}) collective-permute-start(bf16[1,96,1536]{2,1,0:T(8,128)(2,1)S(1)} %get-tuple-element.24.refs_4_), channel_id=1, source_target_pairs={{0,20},{4,16},{8,28},{12,24},{16,4},{20,0},{24,12},{28,8},{1,21},{... | collective-permute-start | bytes 884744 | tf_op jit(solution)/shard_map/ppermute | solution.py:291

commit v4 on v3

--- a/solution.py
+++ b/solution.py
@@ -34,6 +34,12 @@
 
 def pick_kernel(picks, core_rows, pair_dev, waits, staged, *refs):
     mirror_ref, amps_ref, shard_ref = refs[:3]
+    if staged:
+        refs, (own_mirror_ref, mirror_sem) = refs[:-2], refs[-2:]
+        whole = pltpu.make_async_copy(mirror_ref, own_mirror_ref, mirror_sem)
+        whole.start()
+        whole.wait()
+        mirror_ref = own_mirror_ref
     total = len(picks) + (core_rows > 0)
     outs, stages = refs[3 + waits:3 + waits + total], refs[3 + waits + total:-2] if staged else None
     sems, store_sems = refs[-2:]
@@ -93,14 +99,15 @@
     return pl.pallas_call(
         functools.partial(pick_kernel, picks, core_rows, pair_dev, len(earlier), staged),
         out_shape=shapes,
-        in_specs=[SMEM, HBM, HBM] + [ANY] * len(earlier),
+        in_specs=[HBM if staged else SMEM, HBM, HBM] + [ANY] * len(earlier),
         out_specs=[ANY if staged else WHOLE] * len(shapes),
         scratch_shapes=([pltpu.VMEM(shape.shape, shape.dtype) for shape in shapes] if staged else [])
-        + [pltpu.SemaphoreType.DMA((PIECES * sum(len(parts) for parts, _ in picks) + 1,))] * 2,
+        + [pltpu.SemaphoreType.DMA((PIECES * sum(len(parts) for parts, _ in picks) + 1,))] * 2
+        + ([pltpu.SMEM(mirror.shape, mirror.dtype), pltpu.SemaphoreType.DMA] if staged else []),
         compiler_params=pltpu.CompilerParams(vmem_limit_bytes=VMEM_BYTES),
         cost_estimate=FREE,
         name="pick",
-    )(mirror, in_hbm(amps), in_hbm(shard), *earlier)
+    )(in_hbm(mirror) if staged else mirror, in_hbm(amps), in_hbm(shard), *earlier)
 
 
 def extract_kernel(parts, *refs):

time: 113 us -> 112 us (level)
  transfers between devices with their start and end apart: 17 -> 17, of which waited for: 7 -> 7; matrix products, arithmetic and copies ran while one was open for 3% -> 3% of each run, Pallas kernels for 40% -> 41%
where the time goes in v4:
time: 112 us
  Pallas kernels  50.9 us (45%)
  waiting for transfers between devices  40.7 us (36%)
  starting transfers between devices  14.5 us (13%)
  local copies, waits for them, and re-layouts  4.36 us (4%)
    ppermute x17, waiting for transfers between devices, move(): return lax.ppermute(block, axis, [(i, to(i)) for i in range(n)])  40.7 us
    pallas_call x8, Pallas kernels, pick(): pl.pallas_call(functools.partial(pick_kernel, picks, core_rows, pair_dev,...  20.1 us
    ppermute x17, starting transfers between devices, move(): return lax.ppermute(block, axis, [(i, to(i)) for i in range(n)])  14.5 us
    pallas_call x3, Pallas kernels, finish_together(): pl.pallas_call(functools.partial(finish_together_kernel, first, first_row...  13.2 us
    pallas_call x1, Pallas kernels, finish(): pl.pallas_call(functools.partial(finish_kernel, [[length for _, _, length...  12.3 us
    pallas_call x1, Pallas kernels, assemble(): pl.pallas_call(functools.partial(assemble_kernel, (firsts, sides), count)...  2.93 us
    pallas_call x2, Pallas kernels, extract(): pl.pallas_call(functools.partial(extract_kernel, [part[1:] for part in pa...  2.33 us
    unnamed x22, local copies, waits for them, and re-layouts  2.25 us
  transfers between devices with their start and end apart: 17, of which 7 were waited for; matrix products, arithmetic and copies ran while one was open for 3% of the time, Pallas kernels for 41%

profile of v4, /device:TPU:0, one launch (start us, length us, event | category | flops | bytes accessed | tf_op | source)
XLA Modules:
  0.0 111.5 jit_solution(16968782783714862600)
XLA Ops:
  0.0 3.2 %pick.8.refs_3_ = bf16[1,768,1536]{2,1,0:T(8,128)(2,1)} custom-call(s32[64]{0:T(128)} %refs_0_.17, bf16[8,384,1536]{2,1,0:T(8,128)(2,1)} %refs_1_.15, bf16[384,1536]{1,0:T(8,128)(2,1)} %refs_2_.15), custom_call_target="tpu_custom_call" | custom-call | tf_op jit(solution)/shard_map/pick/pallas_call | solution.py:99
  3.3 4.0 %collective-permute-start = (bf16[1,768,1536]{2,1,0:T(8,128)(2,1)}, bf16[1,768,1536]{2,1,0:T(8,128)(2,1)S(1)}, u32[]{:S(2)}, u32[]{:S(2)}) collective-permute-start(bf16[1,768,1536]{2,1,0:T(8,128)(2,1)} %pick.8.refs_3_), channel_id=1, source_target_pairs={{0,24},{4,28},{8,16},{12,20},{16,8},{20,12},{24,0},{28,4},{1,25},{... | collective-permute-start | bytes 7077896 | tf_op jit(solution)/shard_map/ppermute | solution.py:298
  7.2 3.0 %pick.11 = (bf16[1,384,1536]{2,1,0:T(8,128)(2,1)}, bf16[1,192,1536]{2,1,0:T(8,128)(2,1)}) custom-call(s32[64]{0:T(128)} %refs_0_.17, bf16[8,384,1536]{2,1,0:T(8,128)(2,1)} %refs_1_.15, bf16[384,1536]{1,0:T(8,128)(2,1)} %refs_2_.15, bf16[1,768,1536]{2,1,0:T(8,128)(2,1)} %pick.8.refs_3_), custom_call_target="tpu_custom_call" | custom-call | tf_op jit(solution)/shard_map/pick/pallas_call | solution.py:99
  10.3 2.7 %collective-permute-start.4 = (bf16[1,192,1536]{2,1,0:T(8,128)(2,1)}, bf16[1,192,1536]{2,1,0:T(8,128)(2,1)}, u32[]{:S(2)}, u32[]{:S(2)}) collective-permute-start(bf16[1,192,1536]{2,1,0:T(8,128)(2,1)} %get-tuple-element.25.refs_0_), channel_id=1, source_target_pairs={{0,2},{1,3},{2,0},{3,1},{4,6},{5,7},{6,4},{7,5},{8,10},{9,11},{10,... | collective-permute-start | bytes 1769480 | tf_op jit(solution)/shard_map/ppermute | solution.py:298
  12.9 1.6 %collective-permute-start.3 = (bf16[1,192,1536]{2,1,0:T(8,128)(2,1)}, bf16[1,192,1536]{2,1,0:T(8,128)(2,1)S(1)}, u32[]{:S(2)}, u32[]{:S(2)}) collective-permute-start(bf16[1,192,1536]{2,1,0:T(8,128)(2,1)} %get-tuple-element.25.refs_0_), channel_id=1, source_target_pairs={{0,1},{1,0},{2,3},{3,2},{4,5},{5,4},{6,7},{7,6},{8,9},{9,8},{10,11... | collective-permute-start | bytes 1769480 | tf_op jit(solution)/shard_map/ppermute | solution.py:298
  15.2 1.7 %copy.22.refs_6_.refs_5_.refs_7_ = f32[8,384,2]{2,1,0:T(8,128)} copy(f32[8,384,2]{1,0,2:T(8,128)S(1)} %pad_maximum_fusion.1) | data formatting | bytes 49152 | tf_op jit(solution)/shard_map/stack | solution.py:318
  17.0 22.0 %collective-permute-done.4.refs_2_.refs_4_ = bf16[1,192,1536]{2,1,0:T(8,128)(2,1)} collective-permute-done((bf16[1,192,1536]{2,1,0:T(8,128)(2,1)}, bf16[1,192,1536]{2,1,0:T(8,128)(2,1)}, u32[]{:S(2)}, u32[]{:S(2)}) %collective-permute-start.4) | collective-permute-done | bytes 589856 | tf_op jit(solution)/shard_map/ppermute | solution.py:298
  39.1 0.6 collective-permute-start.5
  40.0 1.4 %copy-done = f32[8,384,2]{2,1,0:T(8,128)S(1)} copy-done((f32[8,384,2]{2,1,0:T(8,128)S(1)}, f32[8,384,2]{2,1,0:T(8,128)}, u32[]{:S(2)}) %copy-start) | copy-done | bytes 24600
  41.4 3.5 %pick.12 = (bf16[1,480,1536]{2,1,0:T(8,128)(2,1)}, bf16[1,480,1536]{2,1,0:T(8,128)(2,1)}) custom-call(s32[64]{0:T(128)} %refs_0_.17, bf16[8,384,1536]{2,1,0:T(8,128)(2,1)} %refs_1_.15, bf16[384,1536]{1,0:T(8,128)(2,1)} %refs_2_.15, bf16[1,192,1536]{2,1,0:T(8,128)(2,1)S(1)} %collective-permute-done.3.refs_1_.refs_3_, ...), custom_call_target="tpu_custom_call" | custom-call | tf_op jit(solution)/shard_map/pick/pallas_call | solution.py:99
  44.9 0.6 collective-permute-start.10
  46.0 7.5 %collective-permute-done.5.refs_3_ = bf16[1,192,1536]{2,1,0:T(8,128)(2,1)} collective-permute-done((bf16[1,192,1536]{2,1,0:T(8,128)(2,1)}, bf16[1,192,1536]{2,1,0:T(8,128)(2,1)}, u32[]{:S(2)}, u32[]{:S(2)}) %collective-permute-start.5) | collective-permute-done | bytes 589856 | tf_op jit(solution)/shard_map/ppermute | solution.py:298
  53.5 6.0 %collective-permute-done.refs_3_.refs_0_ = bf16[1,768,1536]{2,1,0:T(8,128)(2,1)S(1)} collective-permute-done((bf16[1,768,1536]{2,1,0:T(8,128)(2,1)}, bf16[1,768,1536]{2,1,0:T(8,128)(2,1)S(1)}, u32[]{:S(2)}, u32[]{:S(2)}) %collective-permute-start) | collective-permute-done | bytes 2359328 | tf_op jit(solution)/shard_map/ppermute | solution.py:298
  59.6 1.3 %extract.2 = bf16[1,384,1536]{2,1,0:T(8,128)(2,1)} custom-call(bf16[1,768,1536]{2,1,0:T(8,128)(2,1)S(1)} %collective-permute-done.refs_3_.refs_0_), custom_call_target="tpu_custom_call" | custom-call | tf_op jit(solution)/shard_map/extract/pallas_call | solution.py:126
  60.8 0.8 copy-done.5
  62.2 1.9 %pick.13.refs_1_ = bf16[1,384,1536]{2,1,0:T(8,128)(2,1)S(1)} custom-call(s32[64]{0:T(128)S(1)} %copy-done.4, bf16[8,384,1536]{2,1,0:T(8,128)(2,1)} %refs_1_.15, bf16[384,1536]{1,0:T(8,128)(2,1)} %refs_2_.15, bf16[1,192,1536]{2,1,0:T(8,128)(2,1)S(1)} %collective-permute-done.3.refs_1_.refs_3_), custom_call_target="tpu_custom_call" | custom-call | tf_op jit(solution)/shard_map/pick/pallas_call | solution.py:99
  64.1 1.7 %collective-permute-done.9.refs_7_ = bf16[1,192,1536]{2,1,0:T(8,128)(2,1)} collective-permute-done((bf16[1,192,1536]{2,1,0:T(8,128)(2,1)}, bf16[1,192,1536]{2,1,0:T(8,128)(2,1)}, u32[]{:S(2)}, u32[]{:S(2)}) %collective-permute-start.9) | collective-permute-done | bytes 589856 | tf_op jit(solution)/shard_map/ppermute | solution.py:298
  65.8 2.9 %assemble.1 = bf16[4,2,192,1536]{3,2,1,0:T(8,128)(2,1)S(1)} custom-call(s32[2]{0:T(128)S(1)} %pad_add_fusion.place_ref, bf16[1,192,1536]{2,1,0:T(8,128)(2,1)} %get-tuple-element.25.refs_0_, bf16[1,192,1536]{2,1,0:T(8,128)(2,1)} %copy-done.2, bf16[1,192,1536]{2,1,0:T(8,128)(2,1)} %collective-permute-done.4.refs_2_.refs_4_, ...), custom_call_target="tpu_custom_call" | custom-call | tf_op jit(solution)/shard_map/assemble/pallas_call | solution.py:152
  68.7 2.0 %pick.15 = (bf16[1,192,1536]{2,1,0:T(8,128)(2,1)S(1)}, bf16[1,192,1536]{2,1,0:T(8,128)(2,1)S(1)}) custom-call(s32[64]{0:T(128)S(1)} %copy-done.4, bf16[8,384,1536]{2,1,0:T(8,128)(2,1)} %refs_1_.15, bf16[384,1536]{1,0:T(8,128)(2,1)} %refs_2_.15, bf16[1,768,1536]{2,1,0:T(8,128)(2,1)S(1)} %collective-permute-done.refs_3_.refs_0_), custom_call_target="tpu_custom_call" | custom-call | tf_op jit(solution)/shard_map/pick/pallas_call | solution.py:99
  70.8 2.0 %collective-permute-start.15 = (bf16[1,192,1536]{2,1,0:T(8,128)(2,1)S(1)}, bf16[1,192,1536]{2,1,0:T(8,128)(2,1)S(1)}, u32[]{:S(2)}, u32[]{:S(2)}) collective-permute-start(bf16[1,192,1536]{2,1,0:T(8,128)(2,1)S(1)} %get-tuple-element.34), channel_id=1, source_target_pairs={{0,12},{4,8},{8,4},{12,0},{16,28},{20,24},{24,20},{28,16},{1,13},{... | collective-permute-start | bytes 1769480 | tf_op jit(solution)/shard_map/ppermute | solution.py:298
  72.8 2.3 %pick.14 = (bf16[1,384,1536]{2,1,0:T(8,128)(2,1)S(1)}, bf16[1,384,1536]{2,1,0:T(8,128)(2,1)S(1)}) custom-call(s32[64]{0:T(128)S(1)} %copy-done.4, bf16[8,384,1536]{2,1,0:T(8,128)(2,1)} %refs_1_.15, bf16[384,1536]{1,0:T(8,128)(2,1)} %refs_2_.15, bf16[1,768,1536]{2,1,0:T(8,128)(2,1)S(1)} %collective-permute-done.refs_3_.refs_0_), custom_call_target="tpu_custom_call" | custom-call | tf_op jit(solution)/shard_map/pick/pallas_call | solution.py:99
  75.1 2.4 %pick.9 = (bf16[1,288,1536]{2,1,0:T(8,128)(2,1)S(1)}, bf16[1,288,1536]{2,1,0:T(8,128)(2,1)S(1)}, bf16[1,96,1536]{2,1,0:T(8,128)(2,1)S(1)}, bf16[1,96,1536]{2,1,0:T(8,128)(2,1)S(1)}) custom-call(s32[64]{0:T(128)S(1)} %copy-done.4, bf16[8,384,1536]{2,1,0:T(8,128)(2,1)} %refs_1_.15, bf16[384,1536]{1,0:T(8,128)(2,1)} %refs_2_.15, ...), custom_call_target="tpu_custom_call" | custom-call | tf_op jit(solution)/shard_map/pick/pallas_call | solution.py:99
  77.5 1.8 %pick.10 = (bf16[1,96,1536]{2,1,0:T(8,128)(2,1)S(1)}, bf16[1,96,1536]{2,1,0:T(8,128)(2,1)S(1)}) custom-call(s32[64]{0:T(128)S(1)} %copy-done.4, bf16[8,384,1536]{2,1,0:T(8,128)(2,1)} %refs_1_.15, bf16[384,1536]{1,0:T(8,128)(2,1)} %refs_2_.15, bf16[1,768,1536]{2,1,0:T(8,128)(2,1)S(1)} %collective-permute-done.refs_3_.refs_0_), custom_call_target="tpu_custom_call" | custom-call | tf_op jit(solution)/shard_map/pick/pallas_call | solution.py:99
  79.4 1.4 %collective-permute-start.16 = (bf16[1,192,1536]{2,1,0:T(8,128)(2,1)S(1)}, bf16[1,192,1536]{2,1,0:T(8,128)(2,1)S(1)}, u32[]{:S(2)}, u32[]{:S(2)}) collective-permute-start(bf16[1,192,1536]{2,1,0:T(8,128)(2,1)S(1)} %get-tuple-element.35), channel_id=1, source_target_pairs={{0,20},{4,16},{8,28},{12,24},{16,4},{20,0},{24,12},{28,8},{1,21},{... | collective-permute-start | bytes 1769480 | tf_op jit(solution)/shard_map/ppermute | solution.py:298
  80.7 12.3 %finish.1 = (bf16[8,384,1536]{2,1,0:T(8,128)(2,1)}, f32[8,128]{1,0:T(8,128)S(1)}) custom-call(s32[8]{0:T(128)S(1)} %select_reduce_fusion.2.refs_5_.slots_ref, bf16[8,384,1536]{2,1,0:T(8,128)(2,1)} %refs_1_.15, bf16[1,384,1536]{2,1,0:T(8,128)(2,1)S(1)} %pick.13.refs_1_, bf16[1,384,1536]{2,1,0:T(8,128)(2,1)} %collective-permute-done.12.refs_2_, ...), custom_call_target="tpu_custom_call" | custom-call | tf_op jit(solution)/shard_map/finish/pallas_call | solution.py:211
  93.0 1.1 extract.3
  94.8 6.6 %finish_together.3.refs_9_ = bf16[8,384,1536]{2,1,0:T(8,128)(2,1)} custom-call(s32[8]{0:T(128)S(1)} %select_reduce_fusion.2.refs_5_.slots_ref, bf16[1,384,1536]{2,1,0:T(8,128)(2,1)S(1)} %get-tuple-element.32.refs_5_.refs_0_, bf16[1,384,1536]{2,1,0:T(8,128)(2,1)S(1)} %get-tuple-element.33.refs_6_.refs_1_, ...), custom_call_target="tpu_custom_call", output_to_operand_aliasing={{}: (8, {})} | custom-call | tf_op jit(solution)/shard_map/finish_together/pallas_call | solution.py:268
  101.4 2.0 %collective-permute-done.15.refs_3_ = bf16[1,192,1536]{2,1,0:T(8,128)(2,1)S(1)} collective-permute-done((bf16[1,192,1536]{2,1,0:T(8,128)(2,1)S(1)}, bf16[1,192,1536]{2,1,0:T(8,128)(2,1)S(1)}, u32[]{:S(2)}, u32[]{:S(2)}) %collective-permute-start.15) | collective-permute-done | bytes 589856 | tf_op jit(solution)/shard_map/ppermute | solution.py:298
  103.4 4.3 %finish_together.4.refs_7_ = bf16[8,384,1536]{2,1,0:T(8,128)(2,1)} custom-call(s32[8]{0:T(128)S(1)} %select_reduce_fusion.2.refs_5_.slots_ref, bf16[1,288,1536]{2,1,0:T(8,128)(2,1)S(1)} %get-tuple-element.26.refs_7_.refs_0_, bf16[1,288,1536]{2,1,0:T(8,128)(2,1)S(1)} %get-tuple-element.27.refs_8_.refs_1_, ...), custom_call_target="tpu_custom_call", output_to_operand_aliasing={{}: (10, {})} | custom-call | tf_op jit(solution)/shard_map/finish_together/pallas_call | solution.py:268
  107.7 0.9 collective-permute-done.1.refs_2_
  108.5 0.6 collective-permute-done.2.refs_3_
  109.2 2.4 %finish_together.5 = bf16[8,384,1536]{2,1,0:T(8,128)(2,1)} custom-call(s32[8]{0:T(128)S(1)} %select_reduce_fusion.2.refs_5_.slots_ref, bf16[1,96,1536]{2,1,0:T(8,128)(2,1)S(1)} %get-tuple-element.21.refs_9_.refs_0_, bf16[1,96,1536]{2,1,0:T(8,128)(2,1)S(1)} %get-tuple-element.22.refs_10_.refs_1_, ...), custom_call_target="tpu_custom_call", output_to_operand_aliasing={{}: (8, {})} | custom-call | tf_op jit(solution)/shard_map/finish_together/pallas_call | solution.py:268
  (56 shorter events, 3.0 us)
Async XLA Ops:
  3.2 11.3 %copy-start.7 = (s32[8,24]{1,0:T(8,128)S(1)}, s32[8,24]{1,0:T(8,128)}, u32[]{:S(2)}) copy-start(s32[8,24]{1,0:T(8,128)} %param.12) | copy-start | bytes 2308
  3.2 11.5 %copy-start.9 = (s32[8,2]{0,1:T(2,128)S(1)}, s32[8,2]{0,1:T(2,128)}, u32[]{:S(2)}) copy-start(s32[8,2]{0,1:T(2,128)} %param.11) | copy-start | bytes 196
  3.2 11.5 %copy-start.8 = (f32[256]{0:T(256)S(1)}, f32[256]{0:T(256)}, u32[]{:S(2)}) copy-start(f32[256]{0:T(256)} %param.13) | copy-start | bytes 3076
  3.3 11.7 %copy-start.6 = (f32[1536]{0:T(1024)S(1)}, f32[1536]{0:T(1024)}, u32[]{:S(2)}) copy-start(f32[1536]{0:T(1024)} %param.14) | copy-start | bytes 18436
  3.3 56.3 %collective-permute-start = (bf16[1,768,1536]{2,1,0:T(8,128)(2,1)}, bf16[1,768,1536]{2,1,0:T(8,128)(2,1)S(1)}, u32[]{:S(2)}, u32[]{:S(2)}) collective-permute-start(bf16[1,768,1536]{2,1,0:T(8,128)(2,1)} %pick.8.refs_3_), channel_id=1, source_target_pairs={{0,24},{4,28},{8,16},{12,20},{16,8},{20,12},{24,0},{28,4},{1,25},{... | collective-permute-start | bytes 7077896 | tf_op jit(solution)/shard_map/ppermute | solution.py:298
  10.2 6.7 %copy-start.3 = (s32[64]{0:T(128)S(1)}, s32[64]{0:T(128)}, u32[]{:S(2)}) copy-start(s32[64]{0:T(128)} %refs_0_.17) | copy-start | bytes 772
  10.2 6.7 %copy-start.10 = (s32[8]{0:T(128)S(1)}, s32[8]{0:T(128)}, u32[]{:S(2)}) copy-start(s32[8]{0:T(128)} %constant.48.clone) | copy-start | bytes 100
  10.3 28.8 %collective-permute-start.4 = (bf16[1,192,1536]{2,1,0:T(8,128)(2,1)}, bf16[1,192,1536]{2,1,0:T(8,128)(2,1)}, u32[]{:S(2)}, u32[]{:S(2)}) collective-permute-start(bf16[1,192,1536]{2,1,0:T(8,128)(2,1)} %get-tuple-element.25.refs_0_), channel_id=1, source_target_pairs={{0,2},{1,3},{2,0},{3,1},{4,6},{5,7},{6,4},{7,5},{8,10},{9,11},{10,... | collective-permute-start | bytes 1769480 | tf_op jit(solution)/shard_map/ppermute | solution.py:298
  12.9 26.7 %collective-permute-start.3 = (bf16[1,192,1536]{2,1,0:T(8,128)(2,1)}, bf16[1,192,1536]{2,1,0:T(8,128)(2,1)S(1)}, u32[]{:S(2)}, u32[]{:S(2)}) collective-permute-start(bf16[1,192,1536]{2,1,0:T(8,128)(2,1)} %get-tuple-element.25.refs_0_), channel_id=1, source_target_pairs={{0,1},{1,0},{2,3},{3,2},{4,5},{5,4},{6,7},{7,6},{8,9},{9,8},{10,11... | collective-permute-start | bytes 1769480 | tf_op jit(solution)/shard_map/ppermute | solution.py:298
  14.5 31.0 %collective-permute-start.6 = (bf16[1,192,1536]{2,1,0:T(8,128)(2,1)}, bf16[1,192,1536]{2,1,0:T(8,128)(2,1)}, u32[]{:S(2)}, u32[]{:S(2)}) collective-permute-start(bf16[1,192,1536]{2,1,0:T(8,128)(2,1)} %get-tuple-element.25.refs_0_), channel_id=1, source_target_pairs={{0,4},{4,0},{8,12},{12,8},{16,20},{20,16},{24,28},{28,24},{1,5},{5... | collective-permute-start | bytes 1769480 | tf_op jit(solution)/shard_map/ppermute | solution.py:298
  39.1 14.4 %collective-permute-start.5 = (bf16[1,192,1536]{2,1,0:T(8,128)(2,1)}, bf16[1,192,1536]{2,1,0:T(8,128)(2,1)}, u32[]{:S(2)}, u32[]{:S(2)}) collective-permute-start(bf16[1,192,1536]{2,1,0:T(8,128)(2,1)} %collective-permute-done.4.refs_2_.refs_4_), channel_id=1, source_target_pairs={{0,1},{1,0},{2,3},{3,2},{4,5},{5,4},{6,7},{7,6},{8,9},{9,8},{10,11... | collective-permute-start | bytes 1769480 | tf_op jit(solution)/shard_map/ppermute | solution.py:298
  39.6 22.6 %copy-start.2 = (bf16[1,192,1536]{2,1,0:T(8,128)(2,1)}, bf16[1,192,1536]{2,1,0:T(8,128)(2,1)S(1)}, u32[]{:S(2)}) copy-start(bf16[1,192,1536]{2,1,0:T(8,128)(2,1)S(1)} %collective-permute-done.3.refs_1_.refs_3_) | copy-start | bytes 1769476
  39.6 21.2 %collective-permute-start.7 = (bf16[1,192,1536]{2,1,0:T(8,128)(2,1)S(1)}, bf16[1,192,1536]{2,1,0:T(8,128)(2,1)S(1)}, u32[]{:S(2)}, u32[]{:S(2)}) collective-permute-start(bf16[1,192,1536]{2,1,0:T(8,128)(2,1)S(1)} %collective-permute-done.3.refs_1_.refs_3_), channel_id=1, source_target_pairs={{0,4},{4,0},{8,12},{12,8},{16,20},{20,16},{24,28},{28,24},{1,5},{5... | collective-permute-start | bytes 1769480 | tf_op jit(solution)/shard_map/ppermute | solution.py:298
  40.0 1.4 %copy-start = (f32[8,384,2]{2,1,0:T(8,128)S(1)}, f32[8,384,2]{2,1,0:T(8,128)}, u32[]{:S(2)}) copy-start(f32[8,384,2]{2,1,0:T(8,128)} %copy.22.refs_6_.refs_5_.refs_7_) | copy-start | bytes 73732
  44.9 48.1 %collective-permute-start.10 = (bf16[1,480,1536]{2,1,0:T(8,128)(2,1)}, bf16[1,480,1536]{2,1,0:T(8,128)(2,1)}, u32[]{:S(2)}, u32[]{:S(2)}) collective-permute-start(bf16[1,480,1536]{2,1,0:T(8,128)(2,1)} %get-tuple-element.28), channel_id=1, source_target_pairs={{0,8},{4,12},{8,0},{12,4},{16,24},{20,28},{24,16},{28,20},{1,9},{5... | collective-permute-start | bytes 4423688 | tf_op jit(solution)/shard_map/ppermute | solution.py:298
  45.5 47.5 %collective-permute-start.11 = (bf16[1,480,1536]{2,1,0:T(8,128)(2,1)}, bf16[1,480,1536]{2,1,0:T(8,128)(2,1)}, u32[]{:S(2)}, u32[]{:S(2)}) collective-permute-start(bf16[1,480,1536]{2,1,0:T(8,128)(2,1)} %get-tuple-element.29), channel_id=1, source_target_pairs={{0,16},{4,20},{8,24},{12,28},{16,0},{20,4},{24,8},{28,12},{1,17},{... | collective-permute-start | bytes 4423688 | tf_op jit(solution)/shard_map/ppermute | solution.py:298
  53.5 8.6 %collective-permute-start.8 = (bf16[1,192,1536]{2,1,0:T(8,128)(2,1)}, bf16[1,192,1536]{2,1,0:T(8,128)(2,1)}, u32[]{:S(2)}, u32[]{:S(2)}) collective-permute-start(bf16[1,192,1536]{2,1,0:T(8,128)(2,1)} %collective-permute-done.4.refs_2_.refs_4_), channel_id=1, source_target_pairs={{0,4},{4,0},{8,12},{12,8},{16,20},{20,16},{24,28},{28,24},{1,5},{5... | collective-permute-start | bytes 1769480 | tf_op jit(solution)/shard_map/ppermute | solution.py:298
  59.6 2.7 %copy-start.4 = (s32[64]{0:T(128)S(1)}, s32[64]{0:T(128)}, u32[]{:S(2)}) copy-start(s32[64]{0:T(128)} %refs_0_.17) | copy-start | bytes 772
  59.6 19.8 %collective-permute-start.12 = (bf16[1,384,1536]{2,1,0:T(8,128)(2,1)}, bf16[1,384,1536]{2,1,0:T(8,128)(2,1)}, u32[]{:S(2)}, u32[]{:S(2)}) collective-permute-start(bf16[1,384,1536]{2,1,0:T(8,128)(2,1)} %get-tuple-element.30), channel_id=1, source_target_pairs={{0,4},{4,0},{8,12},{12,8},{16,20},{20,16},{24,28},{28,24},{1,5},{5... | collective-permute-start | bytes 3538952 | tf_op jit(solution)/shard_map/ppermute | solution.py:298
  60.8 0.8 copy-start.5
  61.6 19.1 %collective-permute-start.13 = (bf16[1,384,1536]{2,1,0:T(8,128)(2,1)}, bf16[1,384,1536]{2,1,0:T(8,128)(2,1)}, u32[]{:S(2)}, u32[]{:S(2)}) collective-permute-start(bf16[1,384,1536]{2,1,0:T(8,128)(2,1)} %extract.2), channel_id=1, source_target_pairs={{0,4},{4,0},{8,12},{12,8},{16,20},{20,16},{24,28},{28,24},{1,5},{5... | collective-permute-start | bytes 3538952 | tf_op jit(solution)/shard_map/ppermute | solution.py:298
  62.2 3.7 %collective-permute-start.9 = (bf16[1,192,1536]{2,1,0:T(8,128)(2,1)}, bf16[1,192,1536]{2,1,0:T(8,128)(2,1)}, u32[]{:S(2)}, u32[]{:S(2)}) collective-permute-start(bf16[1,192,1536]{2,1,0:T(8,128)(2,1)} %collective-permute-done.5.refs_3_), channel_id=1, source_target_pairs={{0,4},{4,0},{8,12},{12,8},{16,20},{20,16},{24,28},{28,24},{1,5},{5... | collective-permute-start | bytes 1769480 | tf_op jit(solution)/shard_map/ppermute | solution.py:298
  70.8 32.6 %collective-permute-start.15 = (bf16[1,192,1536]{2,1,0:T(8,128)(2,1)S(1)}, bf16[1,192,1536]{2,1,0:T(8,128)(2,1)S(1)}, u32[]{:S(2)}, u32[]{:S(2)}) collective-permute-start(bf16[1,192,1536]{2,1,0:T(8,128)(2,1)S(1)} %get-tuple-element.34), channel_id=1, source_target_pairs={{0,12},{4,8},{8,4},{12,0},{16,28},{20,24},{24,20},{28,16},{1,13},{... | collective-permute-start | bytes 1769480 | tf_op jit(solution)/shard_map/ppermute | solution.py:298
  77.5 3.2 %copy-start.1 = (f32[8,384,2]{2,1,0:T(8,128)S(1)}, f32[8,384,2]{2,1,0:T(8,128)}, u32[]{:S(2)}) copy-start(f32[8,384,2]{2,1,0:T(8,128)} %copy.22.refs_6_.refs_5_.refs_7_) | copy-start | bytes 73732
  79.4 24.0 %collective-permute-start.16 = (bf16[1,192,1536]{2,1,0:T(8,128)(2,1)S(1)}, bf16[1,192,1536]{2,1,0:T(8,128)(2,1)S(1)}, u32[]{:S(2)}, u32[]{:S(2)}) collective-permute-start(bf16[1,192,1536]{2,1,0:T(8,128)(2,1)S(1)} %get-tuple-element.35), channel_id=1, source_target_pairs={{0,20},{4,16},{8,28},{12,24},{16,4},{20,0},{24,12},{28,8},{1,21},{... | collective-permute-start | bytes 1769480 | tf_op jit(solution)/shard_map/ppermute | solution.py:298
  94.1 9.3 %collective-permute-start.14 = (bf16[1,192,1536]{2,1,0:T(8,128)(2,1)S(1)}, bf16[1,192,1536]{2,1,0:T(8,128)(2,1)S(1)}, u32[]{:S(2)}, u32[]{:S(2)}) collective-permute-start(bf16[1,192,1536]{2,1,0:T(8,128)(2,1)S(1)} %extract.3), channel_id=1, source_target_pairs={{0,4},{4,0},{8,12},{12,8},{16,20},{20,16},{24,28},{28,24},{1,5},{5... | collective-permute-start | bytes 1769480 | tf_op jit(solution)/shard_map/ppermute | solution.py:298
  94.5 14.0 %collective-permute-start.1 = (bf16[1,96,1536]{2,1,0:T(8,128)(2,1)S(1)}, bf16[1,96,1536]{2,1,0:T(8,128)(2,1)S(1)}, u32[]{:S(2)}, u32[]{:S(2)}) collective-permute-start(bf16[1,96,1536]{2,1,0:T(8,128)(2,1)S(1)} %get-tuple-element.23.refs_3_), channel_id=1, source_target_pairs={{0,12},{4,8},{8,4},{12,0},{16,28},{20,24},{24,20},{28,16},{1,13},{... | collective-permute-start | bytes 884744 | tf_op jit(solution)/shard_map/ppermute | solution.py:298
  94.8 14.4 %collective-permute-start.2 = (bf16[1,96,1536]{2,1,0:T(8,128)(2,1)S(1)}, bf16[1,96,1536]{2,1,0:T(8,128)(2,1)S(1)}, u32[]{:S(2)}, u32[]{:S(2)}) collective-permute-start(bf16[1,96,1536]{2,1,0:T(8,128)(2,1)S(1)} %get-tuple-element.24.refs_4_), channel_id=1, source_target_pairs={{0,20},{4,16},{8,28},{12,24},{16,4},{20,0},{24,12},{28,8},{1,21},{... | collective-permute-start | bytes 884744 | tf_op jit(solution)/shard_map/ppermute | solution.py:298
